TPU v7x, 512 devices: a whole 4x8x8 slice. The times are simulated.
512 devices in a mesh: row: 16 (over y, x_hi), col: 32 (over x_lo, z, core).
Axes of the slice: x: 4 (x_hi: 2, x_lo: 2; x = x_hi * 2 + x_lo), y: 8, z: 8, core: 2. Of those that a mesh axis runs over, the one named last changes fastest.
Arguments:
- matrix: float32 [8, 16, 128, 4, 32, 128], P(None, 'row', None, None, 'col'), may hold values from -26 to 26
Outputs:
- banded: float32 [8, 16, 128, 4, 32, 128], P(None, 'row', None, None, 'col')
- reflectors: float32 [8, 16, 128, 128], P(None, 'row')
All inputs are finite; a program needn't handle non-finite values.
Results may differ from a plain program's by a relative error of at most 0.0003.
Values sent between devices are 32-bit elements; how exact they have to be, the bound alone decides.
No kernel may reach another device: no remote copies, remote signals or barrier semaphores. Data moves between devices by JAX's collectives and lax.ppermute only.
A program may use at most 64 MiB of HBM per device.

v0:
```python
import jax
import jax.numpy as jnp
from jax import lax
from jax.sharding import PartitionSpec as P


def spread(array, axis, root):
    mine = lax.axis_index(axis) == root
    return lax.psum(jnp.where(mine, array, jnp.zeros_like(array)), axis)


def product(first, second):
    return jnp.dot(
        first, second, precision=lax.Precision.HIGHEST, preferred_element_type=jnp.float32
    )


def transposed_product(first, second):
    return lax.dot_general(
        first,
        second,
        (((0,), (0,)), ((), ())),
        precision=lax.Precision.HIGHEST,
        preferred_element_type=jnp.float32,
    )


def cholesky_lower(gram_matrix):
    extent = gram_matrix.shape[0]
    places = jnp.arange(extent)

    def one_column(column, lower):
        picked = jnp.where(places == column, 1.0, 0.0).astype(gram_matrix.dtype)
        target = product(gram_matrix, picked)
        lower_row = product(picked, lower)
        remaining = target - product(lower, lower_row)
        pivot_value = jnp.sum(remaining * picked)
        new_column = jnp.where(places >= column, remaining / jnp.sqrt(pivot_value), 0.0)
        return jnp.where((places == column)[None, :], new_column[:, None], lower)

    return lax.fori_loop(0, extent, one_column, jnp.zeros_like(gram_matrix))


def lower_inverse(lower):
    extent = lower.shape[0]
    places = jnp.arange(extent)
    identity = jnp.eye(extent, dtype=lower.dtype)

    def one_row(index, inverse):
        picked = jnp.where(places == index, 1.0, 0.0).astype(lower.dtype)
        lower_row = product(picked, lower)
        pivot_value = jnp.sum(lower_row * picked)
        new_row = (picked - product(lower_row, inverse)) / pivot_value
        return jnp.where((places == index)[:, None], new_row[None, :], inverse)

    return lax.fori_loop(0, extent, one_row, jnp.zeros_like(identity))


def signed_factor(square):
    extent = square.shape[0]
    places = jnp.arange(extent)

    def elimination(column, carry):
        working, chosen = carry
        pivot_value = working[column, column]
        sign_choice = jnp.where(pivot_value >= 0, -1.0, 1.0).astype(square.dtype)
        shifted = pivot_value - sign_choice
        below_mask = places > column
        multipliers = jnp.where(below_mask, working[:, column] / shifted, 0.0)
        reduced = working - jnp.where(
            below_mask[None, :], multipliers[:, None] * working[column, :][None, :], 0.0
        )
        reduced = jnp.where(
            below_mask[:, None] & (places[None, :] == column), multipliers[:, None], reduced
        )
        reduced = jnp.where(
            (places[:, None] == column) & (places[None, :] == column), shifted, reduced
        )
        chosen = jnp.where(places == column, sign_choice, chosen)
        return (reduced, chosen)

    working, chosen = lax.fori_loop(
        0, extent, elimination, (square, jnp.zeros((extent,), square.dtype))
    )
    upper_factor = jnp.triu(working)
    unit_lower = jnp.tril(working, -1) + jnp.eye(extent, dtype=square.dtype)
    return (upper_factor, chosen, unit_lower)


def compact_factor(upper_factor, chosen, unit_lower):
    scaled = upper_factor * chosen[None, :]
    return -product(scaled, lower_inverse(unit_lower).T)


def place_reflectors(orthonormal, block_index, upper_inverse, unit_lower):
    block_size = unit_lower.shape[0]
    remainder = product(orthonormal, upper_inverse)
    tiled = jnp.tile(unit_lower, (orthonormal.shape[0] // block_size, 1))
    placed = jnp.where((block_index == 1)[:, None], tiled, remainder)
    return jnp.where((block_index == 0)[:, None], 0.0, placed)


def pick_blocks(row_array, column_blocks, col_place, rows_count, cols_count):
    block_size = row_array.shape[1]
    grouped = row_array.reshape(column_blocks, cols_count // rows_count, block_size, block_size)
    picked = lax.dynamic_index_in_dim(grouped, col_place // rows_count, axis=1, keepdims=False)
    return picked.reshape(column_blocks * block_size, block_size)


def on_device(matrix):
    rows_count = lax.axis_size("row")
    cols_count = lax.axis_size("col")
    row_place = lax.axis_index("row")
    col_place = lax.axis_index("col")
    local_blocks = matrix.shape[0]
    block_size = matrix.shape[2]
    column_blocks = matrix.shape[3]
    local_part = matrix.reshape(local_blocks * block_size, column_blocks * block_size)
    row_block = jnp.repeat(jnp.arange(local_blocks) * rows_count + row_place, block_size)
    column_block = jnp.repeat(jnp.arange(column_blocks) * cols_count + col_place, block_size)
    panel_rows = spread(local_part[:, :block_size], "col", 0)
    panel_rows = jnp.where((row_block == 0)[:, None], 0.0, panel_rows)
    second = (
        jnp.where((row_block == 1)[:, None], panel_rows, 0.0)
        .reshape(local_blocks, block_size, block_size)
        .sum(axis=0)
    )
    gram_matrix, second = lax.psum((transposed_product(panel_rows, panel_rows), second), "row")
    factor = cholesky_lower(gram_matrix)
    factor_inverse_t = lower_inverse(factor).T
    upper_factor, chosen, unit_lower = signed_factor(product(second, factor_inverse_t))
    upper_inverse = lower_inverse(upper_factor.T).T
    triangle = compact_factor(upper_factor, chosen, unit_lower)
    ortho_rows = product(panel_rows, factor_inverse_t)
    reflect_rows = place_reflectors(ortho_rows, row_block, upper_inverse, unit_lower)
    reflect_cols = spread(
        pick_blocks(reflect_rows, column_blocks, col_place, rows_count, cols_count),
        "row",
        col_place % rows_count,
    )
    images_rows = lax.psum(product(local_part, reflect_cols), "col")
    images_rows = jnp.where((row_block == 0)[:, None], 0.0, images_rows)
    scaled_rows = product(images_rows, triangle)
    column_sums, coupling = lax.psum(
        (
            transposed_product(local_part, reflect_rows),
            transposed_product(reflect_rows, scaled_rows),
        ),
        "row",
    )
    correction = product(triangle.T, coupling)
    update_rows = scaled_rows - 0.5 * product(reflect_rows, correction)
    images_cols = jnp.where((column_block == 0)[:, None], 0.0, column_sums)
    scaled_cols = product(images_cols, triangle)
    update_cols = scaled_cols - 0.5 * product(reflect_cols, correction)
    updated = (
        local_part - product(reflect_rows, update_cols.T) - product(update_rows, reflect_cols.T)
    )
    band_block = chosen[:, None] * factor.T
    left_rim = jnp.where((row_block == 1)[:, None], jnp.tile(band_block, (local_blocks, 1)), 0.0)
    left_full = jnp.tile(left_rim, (1, column_blocks))
    banded = jnp.where((column_block == 0)[None, :] & (row_block >= 1)[:, None], left_full, updated)
    upper_rim = jnp.where(
        (column_block == 1)[None, :], jnp.tile(band_block.T, (local_blocks, column_blocks)), 0.0
    )
    banded = jnp.where((row_block == 0)[:, None] & (column_block >= 1)[None, :], upper_rim, banded)
    return (
        banded.reshape(matrix.shape),
        reflect_rows.reshape(local_blocks, 1, block_size, block_size),
    )


def solution(mesh):
    in_specs = (P(None, "row", None, None, "col", None),)
    out_specs = (P(None, "row", None, None, "col", None), P(None, "row", None, None))
    return jax.shard_map(
        on_device, mesh=mesh, in_specs=in_specs, out_specs=out_specs, check_vma=False
    )
```

profile of v0, /device:TPU:1, one launch (start us, length us, event | category | flops | bytes accessed | tf_op | source)
XLA Modules:
  0.0 2148.4 jit_solution(2210524660286940591)
XLA Ops:
  7.2 1.8 copy.28
  11.5 234.3 %all-reduce.8.cloned.1.call-done = f32[1024,128]{1,0:T(8,128)} async-done(((f32[1024,128]{1,0:T(8,128)}), f32[1024,128]{1,0:T(8,128)}) %all-reduce.8.cloned.1.call-update) | async-done | bytes 524304 | tf_op jit(solution)/shard_map/psum | solution.py:9
  245.8 1.4 select_select_fusion.5
  247.8 3.1 fusion.70
  251.6 148.3 %all-reduce.16.cloned.1.call-done = (f32[128,128]{1,0:T(8,128)}, f32[128,128]{1,0:T(8,128)}) async-done(((f32[128,128]{1,0:T(8,128)}, f32[128,128]{1,0:T(8,128)}), (f32[128,128]{1,0:T(8,128)}, f32[128,128]{1,0:T(8,128)})) %all-reduce.16.cloned.1.call-update) | async-done | bytes 131088 | tf_op jit(solution)/shard_map/psum | solution.py:128
  400.0 369.5 %while.77 = (s32[]{:T(128)}, f32[128,128]{1,0:T(8,128)S(1)}, f32[128,128]{1,0:T(8,128)}, s32[]{:T(128)}, s32[]{:T(128)}) while((s32[]{:T(128)}, f32[128,128]{1,0:T(8,128)S(1)}, f32[128,128]{1,0:T(8,128)}, s32[]{:T(128)}, s32[]{:T(128)}) %tuple.174), condition=%wide.region_6.7_spmd.clone.clone, body=%wide.region_4.6_spmd.clone.clone.sunk | while | flops 657026 | bytes 332149 | solution.py:41
  400.0 1.0 convolution_bitcast_fusion.10
  408.7 1.0 convolution_bitcast_fusion.10
  411.6 1.0 convolution_bitcast_fusion.10
  423.1 1.0 convolution_bitcast_fusion.10
  426.0 1.0 convolution_bitcast_fusion.10
  437.5 1.0 convolution_bitcast_fusion.10
  452.0 1.0 convolution_bitcast_fusion.10
  463.5 1.0 convolution_bitcast_fusion.10
  466.4 1.0 convolution_bitcast_fusion.10
  477.9 1.0 convolution_bitcast_fusion.10
  480.8 1.0 convolution_bitcast_fusion.10
  492.4 1.0 convolution_bitcast_fusion.10
  506.8 1.0 convolution_bitcast_fusion.10
  518.3 1.0 convolution_bitcast_fusion.10
  521.2 1.0 convolution_bitcast_fusion.10
  532.8 1.0 convolution_bitcast_fusion.10
  535.7 1.0 convolution_bitcast_fusion.10
  547.2 1.0 convolution_bitcast_fusion.10
  561.6 1.0 convolution_bitcast_fusion.10
  573.2 1.0 convolution_bitcast_fusion.10
  576.1 1.0 convolution_bitcast_fusion.10
  587.6 1.0 convolution_bitcast_fusion.10
  590.5 1.0 convolution_bitcast_fusion.10
  602.0 1.0 convolution_bitcast_fusion.10
  616.5 1.0 convolution_bitcast_fusion.10
  628.0 1.0 convolution_bitcast_fusion.10
  630.9 1.0 convolution_bitcast_fusion.10
  642.5 1.0 convolution_bitcast_fusion.10
  645.3 1.0 convolution_bitcast_fusion.10
  656.9 1.0 convolution_bitcast_fusion.10
  671.3 1.0 convolution_bitcast_fusion.10
  682.9 1.0 convolution_bitcast_fusion.10
  685.8 1.0 convolution_bitcast_fusion.10
  697.3 1.0 convolution_bitcast_fusion.10
  700.2 1.0 convolution_bitcast_fusion.10
  711.7 1.0 convolution_bitcast_fusion.10
  726.2 1.0 convolution_bitcast_fusion.10
  737.7 1.0 convolution_bitcast_fusion.10
  740.6 1.0 convolution_bitcast_fusion.10
  752.1 1.0 convolution_bitcast_fusion.10
  755.0 1.0 convolution_bitcast_fusion.10
  769.5 219.3 %while.74 = (s32[]{:T(128)}, f32[128,128]{1,0:T(8,128)S(1)}, f32[128,128]{1,0:T(8,128)S(1)}, s32[]{:T(128)}, s32[]{:T(128)}) while((s32[]{:T(128)}, f32[128,128]{1,0:T(8,128)S(1)}, f32[128,128]{1,0:T(8,128)S(1)}, s32[]{:T(128)}, s32[]{:T(128)}) %tuple.177), condition=%wide.region_9.10_spmd.clone, body=%wide.region_7.9_spmd.clone.sunk | while | flops 443778 | bytes 264548 | solution.py:56
  989.0 290.8 %while.78 = (s32[]{:T(128)}, f32[128,128]{0,1:T(8,128)S(1)}, f32[128]{0:T(128)S(1)}, s32[]{:T(128)}, f32[]{:T(128)}, /*index=5*/f32[]{:T(128)}, f32[]{:T(128)}, s32[]{:T(128)}) while((s32[]{:T(128)}, f32[128,128]{0,1:T(8,128)S(1)}, f32[128]{0:T(128)S(1)}, s32[]{:T(128)}, f32[]{:T(128)}, /*index=5*/f32[]{:T(128)}, ...), condition=%wide.region_11.12_spmd.clone.clone, body=%wide.region_10.11_spmd.clone.clone.sunk | while | flops 115718 | bytes 137385 | solution.py:82
  1279.9 219.3 %while.75 = (s32[]{:T(128)}, f32[128,128]{1,0:T(8,128)S(1)}, f32[128,128]{1,0:T(8,128)S(1)}, s32[]{:T(128)}, s32[]{:T(128)}) while((s32[]{:T(128)}, f32[128,128]{1,0:T(8,128)S(1)}, f32[128,128]{1,0:T(8,128)S(1)}, s32[]{:T(128)}, s32[]{:T(128)}) %tuple.183), condition=%wide.region_14.15_spmd.clone, body=%wide.region_12.14_spmd.clone.sunk | while | flops 443778 | bytes 264548 | solution.py:56
  1500.0 1.0 fusion.63
  1501.9 231.0 %while.76 = (s32[]{:T(128)}, f32[128,128]{1,0:T(8,128)S(1)}, f32[128,128]{1,0:T(8,128)S(1)}, s32[]{:T(128)}, s32[]{:T(128)}) while((s32[]{:T(128)}, f32[128,128]{1,0:T(8,128)S(1)}, f32[128,128]{1,0:T(8,128)S(1)}, s32[]{:T(128)}, s32[]{:T(128)}) %tuple.186), condition=%wide.region_18.19_spmd.clone, body=%wide.region_16.18_spmd.clone.sunk | while | flops 443778 | bytes 264548 | solution.py:56
  1733.6 3.5 convolution_bitcast_fusion.6
  1737.8 4.1 convolution_bitcast_fusion.7
  1741.9 233.6 %all-reduce.12.cloned.1.call-done = f32[1024,128]{1,0:T(8,128)} async-done(((f32[1024,128]{1,0:T(8,128)}), f32[1024,128]{1,0:T(8,128)}) %all-reduce.12.cloned.1.call-update) | async-done | bytes 524304 | tf_op jit(solution)/shard_map/psum | solution.py:141
  1975.5 1.7 fusion.66
  1977.2 1.6 fusion.95
  1979.5 1.6 copy.12
  1982.2 146.8 %all-reduce.14.cloned.1.call-done = (f32[512,128]{1,0:T(8,128)}, f32[128,128]{1,0:T(8,128)}) async-done(((f32[512,128]{1,0:T(8,128)}, f32[128,128]{1,0:T(8,128)}), (f32[512,128]{1,0:T(8,128)}, f32[128,128]{1,0:T(8,128)})) %all-reduce.14.cloned.1.call-update) | async-done | bytes 327696 | tf_op jit(solution)/shard_map/psum | solution.py:144
  2129.0 1.1 fusion.96
  2130.7 1.4 fusion.72
  2132.5 1.8 fusion.97
  2135.1 3.9 fusion.62
  2139.0 2.9 reshape.163
  (3097 shorter events, 1020.1 us)
Async XLA Ops:
  7.2 238.6 %all-reduce.8.cloned.1.call-start = ((), (), s32[]{:S(2)}) async-start(), calls=%async_computation | async-start | bytes 1048576 | tf_op jit(solution)/shard_map/psum | solution.py:9
  9.9 390.1 %all-reduce.16.cloned.1.call-start = ((), (), s32[]{:S(2)}) async-start(), calls=%async_computation.4 | async-start | bytes 262144 | tf_op jit(solution)/shard_map/psum | solution.py:128
  251.0 1482.7 %all-reduce.10.cloned.1.call-start = ((), (), s32[]{:S(2)}) async-start(), calls=%async_computation.1 | async-start | bytes 524288 | tf_op jit(solution)/shard_map/psum | solution.py:9
  400.0 588.8 %copy-start.7 = (f32[128,128]{1,0:T(8,128)S(1)}, f32[128,128]{1,0:T(8,128)}, u32[]{:S(2)}) copy-start(f32[128,128]{1,0:T(8,128)} %get-tuple-element.553) | copy-start | bytes 196612
  769.4 729.8 %copy-start.2 = (f32[1024,128]{1,0:T(8,128)S(1)}, f32[1024,128]{1,0:T(8,128)}, u32[]{:S(2)}) copy-start(f32[1024,128]{1,0:T(8,128)} %all-reduce.8.cloned.1.call-done) | copy-start | bytes 1572868
  1499.9 233.7 %copy-start = (f32[8,1,128,4,1,128]{5,4,3,2,1,0:T(1,128)S(1)}, f32[8,1,128,4,1,128]{5,4,3,2,1,0:T(1,128)}, u32[]{:S(2)}) copy-start(f32[8,1,128,4,1,128]{5,4,3,2,1,0:T(1,128)} %param.11) | copy-start | bytes 6291460
  1501.0 631.5 %copy-start.1 = (f32[1024,128]{1,0:T(8,128)}, f32[1024,128]{1,0:T(8,128)S(1)}, u32[]{:S(2)}) copy-start(f32[1024,128]{1,0:T(8,128)S(1)} %fusion.63) | copy-start | bytes 1572868
  1501.8 473.7 %all-reduce.12.cloned.1.call-start = ((), (), s32[]{:S(2)}) async-start(), calls=%async_computation.2 | async-start | bytes 1048576 | tf_op jit(solution)/shard_map/psum | solution.py:141
  1737.2 391.8 %all-reduce.14.cloned.1.call-start = ((), (), s32[]{:S(2)}) async-start(), calls=%async_computation.3 | async-start | bytes 655360 | tf_op jit(solution)/shard_map/psum | solution.py:144
  1737.8 241.0 %copy-start.5 = (f32[128,128]{0,1:T(8,128)S(1)}, f32[128,128]{0,1:T(8,128)}, u32[]{:S(2)}) copy-start(f32[128,128]{0,1:T(8,128)} %copy.11) | copy-start | bytes 196612
  1978.8 153.3 %copy-start.3 = (f32[512,128]{1,0:T(8,128)S(1)}, f32[512,128]{1,0:T(8,128)}, u32[]{:S(2)}) copy-start(f32[512,128]{1,0:T(8,128)} %all-reduce.10.cloned.1.call-done) | copy-start | bytes 786436
  2130.7 3.7 copy-start.4
  2132.5 2.2 copy-start.6
  2134.3 0.7 copy-start.8
  2134.4 0.7 copy-start.9
  2134.4 0.7 copy-start.10
Sparse Core Ops, SparseCore 0:
  11.5 234.2 all-reduce.7
  251.1 148.8 all-reduce.15
  1502.0 162.1 all-reduce.9
  1737.3 238.1 all-reduce.11
  1978.9 149.9 all-reduce.13
where the time goes:
time: 2170 us; the launch traced here: 2150 us
  matrix products  903 us (42%)
  waiting for transfers between devices  763 us (35%)
  loops' own time  279 us (13%)
  local copies, waits for them, and re-layouts  108 us (5%)
  other arithmetic  81.8 us (4%)
    dot_general x1164, matrix products, product(): jnp.dot(first, second, precision=lax.Precision.HIGHEST, preferred_element...  894 us
    psum x2, waiting for transfers between devices, spread(): return lax.psum(jnp.where(mine, array, jnp.zeros_like(array)), axis)  234 us
    psum x1, waiting for transfers between devices, on_device(): images_rows = lax.psum(product(local_part, reflect_cols), 'col')  234 us
    another operation x1, loops' own time, signed_factor(): lax.fori_loop(0, extent, elimination, (square, jnp.zeros((extent,), squar...  172 us
    psum x1, waiting for transfers between devices, on_device(): lax.psum((transposed_product(panel_rows, panel_rows), second), 'row')  148 us
    psum x1, waiting for transfers between devices, on_device(): lax.psum((transposed_product(local_part, reflect_rows), transposed_produc...  147 us
    another operation x1, loops' own time, cholesky_lower(): return lax.fori_loop(0, extent, one_column, jnp.zeros_like(gram_matrix))  93.9 us
    dynamic_slice x128, local copies, waits for them, and re-layouts, elimination(): pivot_value = working[column, column]  75.3 us
  transfers between devices with their start and end apart: 5, of which 4 were waited for; matrix products, arithmetic and copies ran while one was open for 11% of the time, Pallas kernels for 0%

commit v1 on v0

v1 whole, which is shorter than its diff:
```python
import functools
import jax
import jax.numpy as jnp
from jax import lax
from jax.experimental import pallas as pl
from jax.experimental.pallas import tpu as pltpu
from jax.sharding import PartitionSpec as P

STEP = 32


def product(first, second, first_dim=1, second_dim=0):
    return lax.dot_general(
        first,
        second,
        (((first_dim,), (second_dim,)), ((), ())),
        precision=lax.Precision.HIGHEST,
        preferred_element_type=jnp.float32,
    )


def factor_kernel(
    gram_ref, second_ref, y_ref, m_ref, t_ref, pair_ref, band_ref, ge, x, e, u, j, sg, *, step
):
    size = gram_ref.shape[0]
    lane = lax.broadcasted_iota(jnp.int32, (step, size), 1)
    lane2 = lax.broadcasted_iota(jnp.int32, (step, 2 * size), 1)
    place = lax.broadcasted_iota(jnp.int32, (step, 1), 0)
    eye = (
        lax.broadcasted_iota(jnp.int32, (size, size), 0)
        == lax.broadcasted_iota(jnp.int32, (size, size), 1)
    ).astype(jnp.float32)
    ge[:, :size] = gram_ref[...]
    ge[:, size:] = eye
    x[:size] = second_ref[...]
    x[size:] = eye
    e[...] = eye
    u[...] = jnp.zeros_like(u)
    j[...] = jnp.zeros_like(j)
    for base in range(0, size, step):
        stop = base + step
        g = ge[base:stop, :]
        w = x[base:stop, :]
        ep = e[base:stop, :]
        f = jnp.where(lane - base == place, 1.0, 0.0).astype(jnp.float32)
        band = jnp.zeros((step, size), jnp.float32)
        sgp = jnp.zeros((step, size), jnp.float32)
        for i in range(step):
            at = base + i
            column = g[:, at : at + 1]
            pivot = g[i : i + 1, at : at + 1]
            root = lax.rsqrt(pivot)
            root = root * (1.5 - 0.5 * pivot * root * root)
            row = jnp.where(lane2[:1] >= at, g[i : i + 1, :] * root, 0.0)
            below = place > i
            here = place == i
            g = jnp.where(here, row, g - jnp.where(below, column * root, 0.0) * row)
            r_row = row[:, :size]
            w_pivot = w[i : i + 1, at : at + 1]
            sign = jnp.where(w_pivot >= 0.0, -1.0, 1.0)
            shifted = w_pivot - sign * (pivot * root)
            inverse = 1.0 / shifted
            s_row = sign * r_row
            t_row = jnp.where(lane[:1] >= at, w[i : i + 1, :], 0.0) - s_row
            l = jnp.where(below, w[:, at : at + 1] * inverse, 0.0)
            w = w - jnp.where(here, s_row, l * t_row)
            w = jnp.where((lane == at) & below, l, w)
            e_row = ep[i : i + 1, :]
            ep = ep - l * e_row
            band = jnp.where(here, s_row, band)
            sgp = jnp.where(here, sign * row[:, size:], sgp)
            f_column = f[:, at : at + 1] * inverse
            f = jnp.where(lane == at, f_column, f - f_column * t_row)
        f = jnp.where((lane >= base) & (lane < stop), f, 0.0)
        u_panel = jnp.where(lane >= base + place, w, 0.0)
        x[base:stop, :] = w
        u[base:stop, :size] = u_panel
        u[base:stop, size:] = ep
        e[base:stop, :] = ep
        band_ref[base:stop, :] = band
        sg[base:stop, :] = sgp
        j[base:stop, :] = f
        if stop < size:
            left = jnp.where(lane >= stop, g[:, :size], 0.0)
            d = product(left, g, 0, 0)
            ge[stop:, :] = ge[stop:, :] - d[stop:, :]
        whole = x[...]
        below_rows = lax.broadcasted_iota(jnp.int32, (2 * size, 1), 0) >= stop
        panel = jnp.where(below_rows | (lax.broadcasted_iota(jnp.int32, (2 * size, 1), 0) >= size), product(whole, j[...]), 0.0)
        d = product(panel, u[...])
        x[...] = whole + panel - d[:, :size]
        if stop < size:
            e[stop:, :] = e[stop:, :] - d[stop:size, size:]
        j[base:stop, :] = jnp.zeros((step, size), jnp.float32)
    rows = lax.broadcasted_iota(jnp.int32, (size, size), 0)
    lanes = lax.broadcasted_iota(jnp.int32, (size, size), 1)
    y_ref[...] = jnp.where(rows > lanes, x[:size], 0.0) + eye
    m = x[size:]
    m = jnp.where(rows <= lanes, m, 0.0)
    m_ref[...] = m
    es = product(e[...], sg[...])
    triangle = -product(u[:, :size], es, 1, 1)
    t_ref[...] = triangle
    pair_ref[:size] = product(m, triangle)
    pair_ref[size:] = -product(product(band_ref[...], m), triangle)


def factors(gram, second):
    size = gram.shape[0]
    square = jax.ShapeDtypeStruct((size, size), jnp.float32)
    return pl.pallas_call(
        functools.partial(factor_kernel, step=STEP),
        out_shape=(square, square, square, jax.ShapeDtypeStruct((2 * size, size), jnp.float32), square),
        scratch_shapes=[
            pltpu.VMEM((size, 2 * size), jnp.float32),
            pltpu.VMEM((2 * size, size), jnp.float32),
            pltpu.VMEM((size, size), jnp.float32),
            pltpu.VMEM((size, 2 * size), jnp.float32),
            pltpu.VMEM((size, size), jnp.float32),
            pltpu.VMEM((size, size), jnp.float32),
        ],
        cost_estimate=pl.CostEstimate(flops=1 << 24, bytes_accessed=1 << 22, transcendentals=1 << 12),
    )(gram, second)


def exchange(array, axis):
    return lax.all_to_all(array, axis, 0, 0)


def gather(array, axis):
    count = lax.axis_size(axis)
    return exchange(jnp.broadcast_to(array[None], (count,) + array.shape), axis)


def to_rows(chunk, column_blocks):
    rows_count = lax.axis_size("row")
    cols_count = lax.axis_size("col")
    ratio = cols_count // rows_count
    parts = cols_count // (ratio * column_blocks)
    pairs = []
    for row in range(rows_count):
        for col in range(cols_count):
            block, part = divmod(col, parts)
            source_row = (block // ratio) * parts + part
            source_col = row + rows_count * (block % ratio)
            pairs.append((source_row * cols_count + source_col, row * cols_count + col))
    return lax.ppermute(chunk, ("row", "col"), pairs)


def on_device(matrix):
    rows_count = lax.axis_size("row")
    cols_count = lax.axis_size("col")
    row_place = lax.axis_index("row")
    col_place = lax.axis_index("col")
    local_blocks = matrix.shape[0]
    size = matrix.shape[2]
    column_blocks = matrix.shape[3]
    rows = local_blocks * size
    cols = column_blocks * size
    local_part = matrix.reshape(rows, cols)
    row_block = jnp.repeat(jnp.arange(local_blocks) * rows_count + row_place, size)
    column_block = jnp.repeat(jnp.arange(column_blocks) * cols_count + col_place, size)
    first = local_part[:, :size]
    corner = local_part[:size, :size]
    mine = rows // cols_count
    thin = size // cols_count
    wide = size // rows_count

    panel = jnp.where((row_block == 0)[:, None], 0.0, first)
    found = exchange(
        jnp.concatenate(
            [
                panel.reshape(cols_count, mine, size),
                product(panel, panel, 0, 0).reshape(cols_count, thin, size),
                jnp.where(row_place == 1, corner, 0.0).reshape(cols_count, thin, size),
            ],
            axis=1,
        ),
        "col",
    )[0]
    square = gather(found[mine:], "row").sum(axis=0)
    found = gather(jnp.concatenate([found[:mine], square], axis=0), "col")
    panel_rows = found[:, :mine].reshape(rows, size)
    gram_matrix = found[:, mine : mine + thin].reshape(size, size)
    second = found[:, mine + thin :].reshape(size, size)
    unit_lower, inverse, triangle, pair, band_block = factors(gram_matrix, second)

    strip = local_part[:size].T.reshape(rows_count, mine, size)
    images = product(local_part, panel_rows, 0, 0).reshape(rows_count, mine, size)
    chunks = exchange(jnp.concatenate([images, strip], axis=1), "row")
    image_chunk = chunks[:, :mine].sum(axis=0)
    chunk_block = (row_place * mine) // size * cols_count + col_place
    panel_chunk = chunks[0, mine:]
    other_chunk = chunks[1, mine:]

    scaled = product(jnp.concatenate([image_chunk, other_chunk], axis=1), pair)
    scaled = jnp.where(chunk_block == 0, 0.0, scaled)
    reflect = product(panel_chunk, inverse)
    reflect = jnp.where(chunk_block == 0, 0.0, reflect)
    lower_piece = lax.dynamic_slice_in_dim(unit_lower, (row_place * mine) % size, mine, axis=0)
    reflect = jnp.where(chunk_block == 1, lower_piece, reflect)

    coupling = product(reflect, scaled, 0, 0).reshape(rows_count, wide, size)
    both = jnp.concatenate([scaled, reflect], axis=0)[None]
    both = jnp.broadcast_to(both, (rows_count, 2 * mine, size))
    found = exchange(jnp.concatenate([both, coupling], axis=1), "row")
    scaled_cols = found[:, :mine].reshape(cols, size)
    reflect_cols = found[:, mine : 2 * mine].reshape(cols, size)
    coupling = found[:, 2 * mine :].sum(axis=0)

    scaled = to_rows(scaled, column_blocks)
    found = gather(jnp.concatenate([scaled, coupling], axis=0), "col")
    scaled_rows = found[:, :mine].reshape(rows, size)
    coupling = gather(found[:, mine:].sum(axis=0), "row").reshape(size, size)
    correction = product(triangle, coupling, 0, 0)

    reflect_rows = product(panel_rows, inverse)
    reflect_rows = jnp.where(
        (row_block == 1)[:, None], jnp.tile(unit_lower, (local_blocks, 1)), reflect_rows
    )
    update_cols = scaled_cols - product(reflect_cols, correction)
    updated = local_part - product(
        jnp.concatenate([reflect_rows, scaled_rows], axis=1),
        jnp.concatenate([update_cols, reflect_cols], axis=1),
        1,
        1,
    )
    left_rim = jnp.where(
        (row_block == 1)[:, None], jnp.tile(band_block, (local_blocks, column_blocks)), 0.0
    )
    banded = jnp.where((column_block == 0)[None, :] & (row_block >= 1)[:, None], left_rim, updated)
    upper_rim = jnp.where(
        (column_block == 1)[None, :], jnp.tile(band_block.T, (local_blocks, column_blocks)), 0.0
    )
    banded = jnp.where((row_block == 0)[:, None] & (column_block >= 1)[None, :], upper_rim, banded)
    return (
        banded.reshape(matrix.shape),
        reflect_rows.reshape(local_blocks, 1, size, size),
    )


def solution(mesh):
    in_specs = (P(None, "row", None, None, "col", None),)
    out_specs = (P(None, "row", None, None, "col", None), P(None, "row", None, None))
    return jax.shard_map(
        on_device, mesh=mesh, in_specs=in_specs, out_specs=out_specs, check_vma=False
    )
```

time: 2170 us -> 198 us (0.09)
  matrix products: 903 us -> 12.4 us
  waiting for transfers between devices: 763 us -> 61.9 us
  loops' own time: 279 us -> 0 us
  local copies, waits for them, and re-layouts: 108 us -> 16.4 us
  other arithmetic: 81.8 us -> 4 us
  starting transfers between devices: 0.39 us -> 51 us
  blocking collectives: 0 us -> 31.8 us
    dot_general x1167 -> x9, matrix products: 903 us -> 12.4 us  [product(): lax.dot_general(first, second, (((first_dim,), (second_dim,)), ((), ())),...]
    psum x5 -> x0, waiting for transfers between devices: 763 us -> none  [the longest x2 234 us: spread(): return lax.psum(jnp.where(mine, array, jnp.zeros_like(array)), axis)]
    another operation x5 -> x0, loops' own time: 279 us -> none  [the longest x1 172 us: signed_factor(): lax.fori_loop(0, extent, elimination, (square, jnp.zeros((extent,), squar...]
    dynamic_slice x256 -> x0, local copies, waits for them, and re-layouts: 97.8 us -> none  [the longest x128 75.3 us: elimination(): pivot_value = working[column, column]]
    select_n x900 -> x2, other arithmetic: 74.8 us -> 0.21 us  [the longest x1 0.2 us: on_device(): panel = jnp.where((row_block == 0)[:, None], 0.0, first)]
    all_to_all x0 -> x6, waiting for transfers between devices: none -> 61.9 us  [exchange(): return lax.all_to_all(array, axis, 0, 0)]
    all_to_all x0 -> x6, starting transfers between devices: none -> 43.5 us  [exchange(): return lax.all_to_all(array, axis, 0, 0)]
    all_to_all x0 -> x1, blocking collectives: none -> 31.8 us  [exchange(): return lax.all_to_all(array, axis, 0, 0)]
  transfers between devices with their start and end apart: 5 -> 7, of which waited for: 4 -> 5; matrix products, arithmetic and copies ran while one was open for 11% -> 3% of each run, Pallas kernels for 0% -> 9%
where the time goes in v1:
time: 198 us; the launch traced here: 196 us
  waiting for transfers between devices  61.9 us (31%)
  starting transfers between devices  51 us (26%)
  blocking collectives  31.8 us (16%)
  Pallas kernels  17 us (9%)
  local copies, waits for them, and re-layouts  16.4 us (8%)
  matrix products  12.4 us (6%)
  other arithmetic  4 us (2%)
    all_to_all x6, waiting for transfers between devices, exchange(): return lax.all_to_all(array, axis, 0, 0)  61.9 us
    all_to_all x6, starting transfers between devices, exchange(): return lax.all_to_all(array, axis, 0, 0)  43.5 us
    all_to_all x1, blocking collectives, exchange(): return lax.all_to_all(array, axis, 0, 0)  31.8 us
    pallas_call x1, Pallas kernels, factors(): pl.pallas_call(functools.partial(factor_kernel, step=STEP), out_shape=(sq...  17 us
    dot_general x9, matrix products, product(): lax.dot_general(first, second, (((first_dim,), (second_dim,)), ((), ())),...  12.4 us
    ppermute x1, starting transfers between devices, to_rows(): return lax.ppermute(chunk, ('row', 'col'), pairs)  7.48 us
  transfers between devices with their start and end apart: 7, of which 5 were waited for; matrix products, arithmetic and copies ran while one was open for 3% of the time, Pallas kernels for 9%

profile of v1, /device:TPU:1, one launch (start us, length us, event | category | flops | bytes accessed | tf_op | source)
XLA Modules:
  0.0 195.6 jit_solution(16862620366424686555)
XLA Ops:
  0.7 0.1 broadcast_bitcast_fusion.2
  0.7 1.8 copy.34
  2.5 0.2 slice_select_fusion
  2.7 1.0 fusion.18
  3.7 0.1 pad_maximum_fusion
  3.8 0.0 copy-start
  3.8 31.8 %all_to_all.35 = f32[32,40,128]{2,1,0:T(8,128)S(1)} all-to-all(f32[32,40,128]{2,1,0:T(8,128)S(1)} %pad_maximum_fusion), channel_id=1, replica_groups=mesh['row'=16,'col'=32] {'col'}, dimensions={0} | all-to-all | bytes 1310720 | tf_op jit(solution)/shard_map/all_to_all | solution.py:127
  35.6 0.6 broadcast_in_dim.113
  36.3 9.1 %all-to-all-start.1 = ((f32[16,8,128]{2,1,0:T(8,128)}), f32[16,8,128]{2,1,0:T(8,128)S(1)}, u32[]{:S(2)}, u32[]{:S(2)}) async-start(f32[16,8,128]{2,1,0:T(8,128)} %broadcast_in_dim.113), calls=%async_computation.1 | async-start | bytes 131072 | tf_op jit(solution)/shard_map/all_to_all | solution.py:127
  45.4 9.4 %all-to-all-done.1 = f32[16,8,128]{2,1,0:T(8,128)S(1)} async-done(((f32[16,8,128]{2,1,0:T(8,128)}), f32[16,8,128]{2,1,0:T(8,128)S(1)}, u32[]{:S(2)}, u32[]{:S(2)}) %all-to-all-start.1) | async-done | bytes 65568 | tf_op jit(solution)/shard_map/all_to_all | solution.py:127
  54.8 0.9 broadcast_in_dim.114
  55.7 7.0 %all-to-all-start.2 = ((f32[32,40,128]{2,1,0:T(8,128)}), f32[32,40,128]{2,1,0:T(8,128)S(1)}, u32[]{:S(2)}, u32[]{:S(2)}) async-start(f32[32,40,128]{2,1,0:T(8,128)} %broadcast_in_dim.114), calls=%async_computation.2 | async-start | bytes 1310720 | tf_op jit(solution)/shard_map/all_to_all | solution.py:127
  62.7 0.0 copy-done
  62.7 0.1 copy.20
  62.9 19.0 %all-to-all-done.2 = f32[32,40,128]{2,1,0:T(8,128)S(1)} async-done(((f32[32,40,128]{2,1,0:T(8,128)}), f32[32,40,128]{2,1,0:T(8,128)S(1)}, u32[]{:S(2)}, u32[]{:S(2)}) %all-to-all-start.2) | async-done | bytes 655392 | tf_op jit(solution)/shard_map/all_to_all | solution.py:127
  81.8 0.1 slice.82
  81.9 2.1 %convolution_bitcast_fusion = f32[512,128]{0,1:T(8,128)} fusion(f32[1024,128]{1,0:T(8,128)S(1)} %bitcast.91, f32[128,8,4,128]{3,2,1,0:T(4,128)S(1)} %bitcast.86), kind=kOutput, calls=%fused_computation.7 | convolution fusion | flops 805306368 | bytes 2883584 | tf_op jit(solution)/shard_map/dot_general | solution.py:13
  84.0 1.8 copy.19
  85.8 1.8 pad_maximum_fusion.2
  87.5 4.4 %all-to-all-start.3 = ((f32[16,64,128]{2,1,0:T(8,128)}), f32[16,64,128]{2,1,0:T(8,128)}, u32[]{:S(2)}, u32[]{:S(2)}) async-start(f32[16,64,128]{2,1,0:T(8,128)} %pad_maximum_fusion.2), calls=%async_computation.3 | async-start | bytes 1048576 | tf_op jit(solution)/shard_map/all_to_all | solution.py:127
  92.0 0.7 fusion.16
  92.7 17.0 %shard_map.30 = (f32[128,128]{1,0:T(8,128)}, f32[128,128]{1,0:T(8,128)}, f32[128,128]{1,0:T(8,128)}, f32[256,128]{1,0:T(8,128)}, f32[128,128]{1,0:T(8,128)}) custom-call(f32[128,128]{1,0:T(8,128)} %bitcast.108, f32[128,128]{1,0:T(8,128)} %bitcast.107), custom_call_target="tpu_custom_call" | custom-call | flops 16777216 | bytes 4194304 | tf_op jit(solution)/shard_map/pallas_call | solution.py:111
  109.7 0.0 all-to-all-done.3
  109.7 0.7 slice_bitcast_fusion.2
  110.4 1.0 slice_reduce_fusion
  111.4 1.1 convolution_select_fusion.2
  112.5 1.0 fusion.2
  113.5 0.3 convolution_bitcast_fusion.1
  113.9 0.0 copy-start.5
  113.9 0.0 copy-start.7
  113.9 0.9 pad_maximum_fusion.1
  114.7 8.8 %all-to-all-start.4 = ((f32[16,72,128]{2,1,0:T(8,128)}), f32[16,72,128]{2,1,0:T(8,128)S(1)}, u32[]{:S(2)}, u32[]{:S(2)}) async-start(f32[16,72,128]{2,1,0:T(8,128)} %pad_maximum_fusion.1), calls=%async_computation.4 | async-start | bytes 1179648 | tf_op jit(solution)/shard_map/all_to_all | solution.py:127
  123.6 0.1 broadcast_bitcast_fusion.5
  123.7 7.5 %collective-permute-start = (f32[32,128]{1,0:T(8,128)S(1)}, f32[32,128]{1,0:T(8,128)S(1)}, u32[]{:S(2)}, u32[]{:S(2)}) collective-permute-start(f32[32,128]{1,0:T(8,128)S(1)} %convolution_select_fusion.2), channel_id=1, source_target_pairs={{0,0},{32,1},{64,2},{96,3},{16,4},{48,5},{80,6},{112,7},{128,8},{1... | collective-permute-start | bytes 49160 | tf_op jit(solution)/shard_map/ppermute | solution.py:147
  131.2 10.0 %all-to-all-done.4 = f32[16,72,128]{2,1,0:T(8,128)S(1)} async-done(((f32[16,72,128]{2,1,0:T(8,128)}), f32[16,72,128]{2,1,0:T(8,128)S(1)}, u32[]{:S(2)}, u32[]{:S(2)}) %all-to-all-start.4) | async-done | bytes 589856 | tf_op jit(solution)/shard_map/all_to_all | solution.py:127
  141.2 0.0 collective-permute-done
  141.2 1.0 broadcast_in_dim.123
  142.2 0.1 copy-done.2
  142.2 9.3 %all-to-all-start.5 = ((f32[32,40,128]{2,1,0:T(8,128)}), f32[32,40,128]{2,1,0:T(8,128)S(1)}, u32[]{:S(2)}, u32[]{:S(2)}) async-start(f32[32,40,128]{2,1,0:T(8,128)} %broadcast_in_dim.123), calls=%async_computation.5 | async-start | bytes 1310720 | tf_op jit(solution)/shard_map/all_to_all | solution.py:127
  151.5 0.6 broadcast_bitcast_fusion.3
  152.1 0.6 broadcast_bitcast_fusion.4
  152.7 0.1 broadcast_bitcast_fusion
  152.8 0.1 broadcast_bitcast_fusion.1
  152.9 0.0 copy-done.5
  152.9 0.7 copy.18
  153.6 0.0 copy-done.4
  153.6 1.4 convolution_select_fusion
  155.0 15.5 %all-to-all-done.5 = f32[32,40,128]{2,1,0:T(8,128)S(1)} async-done(((f32[32,40,128]{2,1,0:T(8,128)}), f32[32,40,128]{2,1,0:T(8,128)S(1)}, u32[]{:S(2)}, u32[]{:S(2)}) %all-to-all-start.5) | async-done | bytes 655392 | tf_op jit(solution)/shard_map/all_to_all | solution.py:127
  170.5 0.7 broadcast_in_dim.124
  171.2 4.9 %all-to-all-start.6 = ((f32[16,8,128]{2,1,0:T(8,128)}), f32[16,8,128]{2,1,0:T(8,128)}, u32[]{:S(2)}, u32[]{:S(2)}) async-start(f32[16,8,128]{2,1,0:T(8,128)} %broadcast_in_dim.124), calls=%async_computation.6 | async-start | bytes 131072 | tf_op jit(solution)/shard_map/all_to_all | solution.py:127
  176.1 1.1 fusion.17
  177.2 0.1 copy.21
  177.4 0.1 copy.22
  177.5 8.1 %all-to-all-done.6 = f32[16,8,128]{2,1,0:T(8,128)} async-done(((f32[16,8,128]{2,1,0:T(8,128)}), f32[16,8,128]{2,1,0:T(8,128)}, u32[]{:S(2)}, u32[]{:S(2)}) %all-to-all-start.6) | async-done | bytes 65568 | tf_op jit(solution)/shard_map/all_to_all | solution.py:127
  185.6 1.2 fusion.9
  186.8 0.4 convolution_subtract_fusion
  187.2 0.0 slice-start
  187.2 0.0 copy-start.3
  187.2 0.0 copy-start.8
  187.3 0.0 copy-start.9
  187.3 1.2 tile.12
  188.5 0.3 tile.14
  188.8 3.9 %fusion.1 = f32[1024,512]{1,0:T(8,128)} fusion(f32[128,8,4,128]{3,2,1,0:T(4,128)S(1)} %bitcast.90, f32[128,8,4,128]{3,2,1,0:T(4,128)S(1)} %bitcast.89, f32[1024,128]{1,0:T(8,128)S(1)} %bitcast.95, f32[1024,128]{1,0:T(8,128)S(1)} %copy-done.3, pred[1024]{0:T(1024)(128)(4,1)S(1)} %broadcast_bitcast_fusion, pred[512]{0:T(512)(128)(4,1)S(1)} %copy-done.8, ...), kind=kOutput, calls=%fused_computation.2 | convolution fusion | flops 1614675968 | bytes 9966080 | tf_op jit(solution)/shard_map/dot_general | solution.py:13
  192.7 2.9 %reshape.124 = f32[8,1,128,4,1,128]{5,3,2,0,4,1:T(4,128)} reshape(f32[1024,512]{1,0:T(8,128)} %fusion.1) | data formatting | bytes 4194304 | tf_op jit(solution)/shard_map/reshape | solution.py:237
  (27 shorter events, 0.3 us)
Async XLA Ops:
  3.8 58.9 %copy-start = (f32[8,1,128,4,1,128]{5,4,3,2,1,0:T(1,128)S(1)}, f32[8,1,128,4,1,128]{5,4,3,2,1,0:T(1,128)}, u32[]{:S(2)}) copy-start(f32[8,1,128,4,1,128]{5,4,3,2,1,0:T(1,128)} %param.1) | copy-start | bytes 6291460
  36.3 18.5 %all-to-all-start.1 = ((f32[16,8,128]{2,1,0:T(8,128)}), f32[16,8,128]{2,1,0:T(8,128)S(1)}, u32[]{:S(2)}, u32[]{:S(2)}) async-start(f32[16,8,128]{2,1,0:T(8,128)} %broadcast_in_dim.113), calls=%async_computation.1 | async-start | bytes 131072 | tf_op jit(solution)/shard_map/all_to_all | solution.py:127
  55.7 26.1 %all-to-all-start.2 = ((f32[32,40,128]{2,1,0:T(8,128)}), f32[32,40,128]{2,1,0:T(8,128)S(1)}, u32[]{:S(2)}, u32[]{:S(2)}) async-start(f32[32,40,128]{2,1,0:T(8,128)} %broadcast_in_dim.114), calls=%async_computation.2 | async-start | bytes 1310720 | tf_op jit(solution)/shard_map/all_to_all | solution.py:127
  87.5 22.1 %all-to-all-start.3 = ((f32[16,64,128]{2,1,0:T(8,128)}), f32[16,64,128]{2,1,0:T(8,128)}, u32[]{:S(2)}, u32[]{:S(2)}) async-start(f32[16,64,128]{2,1,0:T(8,128)} %pad_maximum_fusion.2), calls=%async_computation.3 | async-start | bytes 1048576 | tf_op jit(solution)/shard_map/all_to_all | solution.py:127
  113.9 39.0 %copy-start.5 = (f32[128,128]{1,0:T(8,128)S(1)}, f32[128,128]{1,0:T(8,128)}, u32[]{:S(2)}) copy-start(f32[128,128]{1,0:T(8,128)} %get-tuple-element.7) | copy-start | bytes 196612
  113.9 39.7 %copy-start.7 = (f32[128,128]{1,0:T(8,128)S(1)}, f32[128,128]{1,0:T(8,128)}, u32[]{:S(2)}) copy-start(f32[128,128]{1,0:T(8,128)} %get-tuple-element.8) | copy-start | bytes 196612
  114.7 38.9 %copy-start.4 = (f32[128,128]{1,0:T(8,128)S(1)}, f32[128,128]{1,0:T(8,128)}, u32[]{:S(2)}) copy-start(f32[128,128]{1,0:T(8,128)} %get-tuple-element.9) | copy-start | bytes 196612
  114.7 26.4 %all-to-all-start.4 = ((f32[16,72,128]{2,1,0:T(8,128)}), f32[16,72,128]{2,1,0:T(8,128)S(1)}, u32[]{:S(2)}, u32[]{:S(2)}) async-start(f32[16,72,128]{2,1,0:T(8,128)} %pad_maximum_fusion.1), calls=%async_computation.4 | async-start | bytes 1179648 | tf_op jit(solution)/shard_map/all_to_all | solution.py:127
  123.7 17.5 %collective-permute-start = (f32[32,128]{1,0:T(8,128)S(1)}, f32[32,128]{1,0:T(8,128)S(1)}, u32[]{:S(2)}, u32[]{:S(2)}) collective-permute-start(f32[32,128]{1,0:T(8,128)S(1)} %convolution_select_fusion.2), channel_id=1, source_target_pairs={{0,0},{32,1},{64,2},{96,3},{16,4},{48,5},{80,6},{112,7},{128,8},{1... | collective-permute-start | bytes 49160 | tf_op jit(solution)/shard_map/ppermute | solution.py:147
  141.2 1.1 copy-start.2
  142.2 28.3 %all-to-all-start.5 = ((f32[32,40,128]{2,1,0:T(8,128)}), f32[32,40,128]{2,1,0:T(8,128)S(1)}, u32[]{:S(2)}, u32[]{:S(2)}) async-start(f32[32,40,128]{2,1,0:T(8,128)} %broadcast_in_dim.123), calls=%async_computation.5 | async-start | bytes 1310720 | tf_op jit(solution)/shard_map/all_to_all | solution.py:127
  170.5 16.7 %copy-start.1 = (f32[32,40,128]{2,1,0:T(8,128)}, f32[32,40,128]{2,1,0:T(8,128)S(1)}, u32[]{:S(2)}) copy-start(f32[32,40,128]{2,1,0:T(8,128)S(1)} %all-to-all-done.5) | copy-start | bytes 1966084
  171.2 14.3 %all-to-all-start.6 = ((f32[16,8,128]{2,1,0:T(8,128)}), f32[16,8,128]{2,1,0:T(8,128)}, u32[]{:S(2)}, u32[]{:S(2)}) async-start(f32[16,8,128]{2,1,0:T(8,128)} %broadcast_in_dim.124), calls=%async_computation.6 | async-start | bytes 131072 | tf_op jit(solution)/shard_map/all_to_all | solution.py:127
  185.6 2.9 %copy-start.6 = (f32[128,128]{1,0:T(8,128)S(1)}, f32[128,128]{1,0:T(8,128)}, u32[]{:S(2)}) copy-start(f32[128,128]{1,0:T(8,128)} %get-tuple-element.7) | copy-start | bytes 196612
  187.2 1.5 slice-start
  187.2 1.5 copy-start.3
  187.2 1.5 copy-start.8
  187.3 1.5 copy-start.9

commit v2 on v1

v2 whole, which is shorter than its diff:
```python
import functools
import jax
import jax.numpy as jnp
from jax import lax
from jax.experimental import pallas as pl
from jax.experimental.pallas import tpu as pltpu
from jax.sharding import PartitionSpec as P

STEP = 32


def product(first, second, first_dim=1, second_dim=0):
    return lax.dot_general(
        first,
        second,
        (((first_dim,), (second_dim,)), ((), ())),
        precision=lax.Precision.HIGHEST,
        preferred_element_type=jnp.float32,
    )


def halves(array):
    high = array.astype(jnp.bfloat16)
    return high, (array - high.astype(jnp.float32)).astype(jnp.bfloat16)


def passes(first, second, first_dim=1, second_dim=0):
    dims = (((first_dim,), (second_dim,)), ((), ()))

    def one(a, b):
        return lax.dot_general(a, b, dims, preferred_element_type=jnp.float32)

    return one(first[0], second[0]) + (one(first[0], second[1]) + one(first[1], second[0]))


def factor_kernel(own_ref, other_ref, out_ref, ge, x, e, u, j, sg, bd, *, step):
    size = out_ref.shape[1]
    thin = size // own_ref.shape[0]
    mine = own_ref.shape[1] - 2 * thin
    lane = lax.broadcasted_iota(jnp.int32, (step, size), 1)
    lane2 = lax.broadcasted_iota(jnp.int32, (step, 2 * size), 1)
    place = lax.broadcasted_iota(jnp.int32, (step, 1), 0)
    eye = (
        lax.broadcasted_iota(jnp.int32, (size, size), 0)
        == lax.broadcasted_iota(jnp.int32, (size, size), 1)
    ).astype(jnp.float32)
    both = own_ref[:, mine:, :] + other_ref[:, mine:, :]
    ge[:, :size] = both[:, :thin].reshape(size, size)
    x[:size] = both[:, thin:].reshape(size, size)
    ge[:, size:] = eye
    x[size:] = eye
    e[...] = eye
    u[...] = jnp.zeros_like(u)
    j[...] = jnp.zeros_like(j)
    for base in range(0, size, step):
        stop = base + step
        g = ge[base:stop, :]
        w = x[base:stop, :]
        ep = e[base:stop, :]
        f = jnp.where(lane - base == place, 1.0, 0.0).astype(jnp.float32)
        band = jnp.zeros((step, size), jnp.float32)
        sgp = jnp.zeros((step, size), jnp.float32)
        for i in range(step):
            at = base + i
            column = g[:, at : at + 1]
            pivot = g[i : i + 1, at : at + 1]
            root = lax.rsqrt(pivot)
            root = root * (1.5 - 0.5 * pivot * root * root)
            row = jnp.where(lane2[:1] >= at, g[i : i + 1, :] * root, 0.0)
            below = place > i
            here = place == i
            g = jnp.where(here, row, g - jnp.where(below, column * root, 0.0) * row)
            r_row = row[:, :size]
            w_pivot = w[i : i + 1, at : at + 1]
            sign = jnp.where(w_pivot >= 0.0, -1.0, 1.0)
            shifted = w_pivot - sign * (pivot * root)
            inverse = 1.0 / shifted
            s_row = sign * r_row
            t_row = jnp.where(lane[:1] >= at, w[i : i + 1, :], 0.0) - s_row
            l = jnp.where(below, w[:, at : at + 1] * inverse, 0.0)
            w = w - jnp.where(here, s_row, l * t_row)
            w = jnp.where((lane == at) & below, l, w)
            e_row = ep[i : i + 1, :]
            ep = ep - l * e_row
            band = jnp.where(here, s_row, band)
            sgp = jnp.where(here, sign * row[:, size:], sgp)
            f_column = f[:, at : at + 1] * inverse
            f = jnp.where(lane == at, f_column, f - f_column * t_row)
        f = jnp.where((lane >= base) & (lane < stop), f, 0.0)
        u_panel = jnp.where(lane >= base + place, w, 0.0)
        x[base:stop, :] = w
        u[base:stop, :size] = u_panel
        u[base:stop, size:] = ep
        e[base:stop, :] = ep
        bd[base:stop, :] = band
        sg[base:stop, :] = sgp
        j[base:stop, :] = f
        if stop < size:
            left = jnp.where(lane >= stop, g[:, :size], 0.0)
            d = product(left, g, 0, 0)
            ge[stop:, :] = ge[stop:, :] - d[stop:, :]
        whole = x[...]
        below_rows = lax.broadcasted_iota(jnp.int32, (2 * size, 1), 0) >= stop
        panel = jnp.where(below_rows | (lax.broadcasted_iota(jnp.int32, (2 * size, 1), 0) >= size), product(whole, j[...]), 0.0)
        d = product(panel, u[...])
        x[...] = whole + panel - d[:, :size]
        if stop < size:
            e[stop:, :] = e[stop:, :] - d[stop:size, size:]
        j[base:stop, :] = jnp.zeros((step, size), jnp.float32)
    rows = lax.broadcasted_iota(jnp.int32, (size, size), 0)
    lanes = lax.broadcasted_iota(jnp.int32, (size, size), 1)
    m = jnp.where(rows <= lanes, x[size:], 0.0)
    es = product(e[...], sg[...])
    triangle = -product(u[:, :size], es, 1, 1)
    out_ref[:size] = product(m, triangle)
    out_ref[size : 2 * size] = -product(product(bd[...], m), triangle)
    out_ref[2 * size : 3 * size] = m
    out_ref[3 * size : 4 * size] = jnp.where(rows > lanes, x[:size], 0.0) + eye
    out_ref[4 * size : 5 * size] = triangle
    out_ref[5 * size :] = bd[...]


def open_kernel(place, own_ref, other_ref, out_ref):
    size = own_ref.shape[1]
    count, extent, _ = out_ref.shape
    thin = size // count
    mine = extent - 2 * thin
    core = place[1]
    panel = jnp.where(core == 0, own_ref[...], other_ref[...])
    second = jnp.where((place[0] == 1) & (core == 0), panel[:size], 0.0)
    index = lax.broadcasted_iota(jnp.int32, panel.shape, 0)
    panel = jnp.where((index < size) & (place[0] == 0) & (core == 0), 0.0, panel)
    out_ref[:, :mine, :] = panel.reshape(count, mine, size)
    out_ref[:, mine : mine + thin, :] = product(panel, panel, 0, 0).reshape(count, thin, size)
    out_ref[:, mine + thin :, :] = second.reshape(count, thin, size)


def strip_kernel(place, strip_ref, out_ref):
    size = strip_ref.shape[2]
    count, mine, _ = out_ref.shape
    each = size // mine
    for b in range(strip_ref.shape[1]):
        turned = strip_ref[:, b, :].T
        if b == 0:
            turned = jnp.where(place[1] == 0, 0.0, turned)
        out_ref[b * each : (b + 1) * each] = turned.reshape(each, mine, size)


def image_kernel(place, own_ref, other_ref, matrix_ref, chunk_ref, out_ref):
    size = own_ref.shape[2]
    count, extent, _ = out_ref.shape
    mine = extent // 2
    each = size // mine
    own = own_ref[:, :mine, :].reshape(-1, size)
    other = other_ref[:, :mine, :].reshape(-1, size)
    even = place[1] % 2 == 0
    panel = jnp.concatenate([jnp.where(even, own, other), jnp.where(even, other, own)], axis=0)
    high, low = halves(panel.T)
    matrix_high, matrix_low = halves(matrix_ref[...])
    image = jnp.dot(
        jnp.concatenate([high, low], axis=0), matrix_high, preferred_element_type=jnp.float32
    )
    image = image[:size] + (
        image[size:] + jnp.dot(high, matrix_low, preferred_element_type=jnp.float32)
    )
    for b in range(matrix_ref.shape[1] // size):
        turned = image[:, b * size : (b + 1) * size].T
        out_ref[b * each : (b + 1) * each, :mine, :] = turned.reshape(each, mine, size)
    out_ref[:, mine:, :] = jnp.broadcast_to(chunk_ref[...][None], (count, mine, size))


def middle_kernel(place, found_ref, panel_ref, second_ref, factors_ref, out_ref):
    size = factors_ref.shape[1]
    count, extent, _ = found_ref.shape
    mine = extent // 2
    wide = size // count
    image = found_ref[0, :mine, :]
    for p in range(1, count):
        image = image + found_ref[p, :mine, :]
    block = (place[0] * mine) // size * place[3] + place[1]
    both = jnp.concatenate([image, second_ref[...]], axis=1)
    scaled = product(both, factors_ref[: 2 * size])
    scaled = jnp.where(block == 0, 0.0, scaled)
    reflect = product(panel_ref[...], factors_ref[2 * size : 3 * size])
    offset = pl.multiple_of(3 * size + (place[0] * mine) % size, mine)
    reflect = jnp.where(block == 1, factors_ref[pl.ds(offset, mine), :], reflect)
    reflect = jnp.where(block == 0, 0.0, reflect)
    coupling = product(reflect, scaled, 0, 0)
    out_ref[:, :mine, :] = jnp.broadcast_to(scaled[None], (count, mine, size))
    out_ref[:, mine:, :] = coupling.reshape(count, wide, size)


def close_kernel(
    place,
    matrix_ref,
    cols_ref,
    reflect_cols_ref,
    own_ref,
    other_ref,
    coupling_ref,
    reflect_ref,
    factors_ref,
    out_ref,
    high,
    low,
):
    step = pl.program_id(0)
    size = factors_ref.shape[1]
    mine = cols_ref.shape[1] - coupling_ref.shape[1]
    blocks = out_ref.shape[1]
    extent = out_ref.shape[0]
    ratio = extent // size
    each = extent // mine

    @pl.when(step == 0)
    def _():
        coupling = coupling_ref[...].reshape(size, size)
        correction = product(factors_ref[4 * size : 5 * size], coupling, 0, 0)
        reflect_cols = reflect_cols_ref[...]
        scaled_cols = cols_ref[:, :mine, :].reshape(-1, size)
        update = scaled_cols - passes(halves(reflect_cols), halves(correction))
        right = halves(jnp.concatenate([update, reflect_cols], axis=1))
        high[...] = right[0]
        low[...] = right[1]

    pairs = own_ref.shape[0]
    first = pl.multiple_of((step * each) % pairs, each)
    here = (step * each) // pairs == place[1] % 2
    scaled = jnp.where(
        here, own_ref[pl.ds(first, each), :mine, :], other_ref[pl.ds(first, each), :mine, :]
    )
    rows = pl.ds(pl.multiple_of(step * extent, extent), extent)
    left = jnp.concatenate([reflect_ref[rows, :], scaled.reshape(extent, size)], axis=1)
    value = matrix_ref[rows, :] - passes(halves(left), (high[...], low[...]), 1, 1)
    band = factors_ref[5 * size :]
    for h in range(ratio):
        row_block = (step * ratio + h) * place[2] + place[0]
        for b in range(blocks):
            column_block = b * place[3] + place[1]
            part = slice(h * size, (h + 1) * size)
            tile = value[part, b * size : (b + 1) * size]
            if b == 0:
                rim = jnp.where(row_block == 1, band, 0.0)
                tile = jnp.where((column_block == 0) & (row_block >= 1), rim, tile)
            if h == 0:
                rim = jnp.where(column_block == 1, band.T, 0.0) if b == 0 else jnp.zeros_like(band)
                tile = jnp.where((row_block == 0) & (column_block >= 1), rim, tile)
            out_ref[part, b, :] = tile


def cost(flops, moved):
    return pl.CostEstimate(flops=flops, bytes_accessed=moved, transcendentals=0)


def struct(*shape):
    return jax.ShapeDtypeStruct(shape, jnp.float32)


SCALARS = pl.BlockSpec(memory_space=pltpu.SMEM)
WHOLE = pl.BlockSpec(memory_space=pltpu.VMEM)
ROOM = pltpu.CompilerParams(vmem_limit_bytes=16 << 20)


def factors(own, other):
    size = own.shape[2]
    return pl.pallas_call(
        functools.partial(factor_kernel, step=STEP),
        out_shape=struct(6 * size, size),
        scratch_shapes=[
            pltpu.VMEM((size, 2 * size), jnp.float32),
            pltpu.VMEM((2 * size, size), jnp.float32),
            pltpu.VMEM((size, size), jnp.float32),
            pltpu.VMEM((size, 2 * size), jnp.float32),
            pltpu.VMEM((size, size), jnp.float32),
            pltpu.VMEM((size, size), jnp.float32),
            pltpu.VMEM((size, size), jnp.float32),
        ],
        compiler_params=ROOM,
        cost_estimate=cost(1 << 28, 1 << 25),
    )(own, other)


def exchange(array):
    return lax.all_to_all(array, "row", 0, 0)


def same_core(array):
    count = lax.axis_size("col")
    groups = [list(range(core, count, 2)) for core in range(2)]
    return lax.all_to_all(array, "col", 0, 0, axis_index_groups=groups)


def flip(array):
    count = lax.axis_size("col")
    return lax.ppermute(array, "col", [(i, i ^ 1) for i in range(count)])


def to_all(array, count):
    return jnp.broadcast_to(array[None], (count,) + array.shape)


def to_rows(chunk, column_blocks):
    rows_count = lax.axis_size("row")
    cols_count = lax.axis_size("col")
    ratio = cols_count // rows_count
    parts = cols_count // (ratio * column_blocks)
    pairs = []
    for row in range(rows_count):
        for col in range(cols_count):
            block, part = divmod(col % 2 * (cols_count // 2) + col // 2, parts)
            source_row = (block // ratio) * parts + part
            source_col = row + rows_count * (block % ratio)
            pairs.append((source_row * cols_count + source_col, row * cols_count + col))
    return lax.ppermute(chunk, ("row", "col"), pairs)


def on_device(matrix):
    rows_count = lax.axis_size("row")
    cols_count = lax.axis_size("col")
    row_place = lax.axis_index("row")
    col_place = lax.axis_index("col")
    local_blocks = matrix.shape[0]
    size = matrix.shape[2]
    column_blocks = matrix.shape[3]
    rows = local_blocks * size
    cols = column_blocks * size
    ratio = cols_count // rows_count
    pairs = cols_count // 2
    mine = rows // cols_count
    thin = size // pairs
    wide = size // rows_count
    table = matrix.reshape(rows, column_blocks, size)
    local_part = matrix.reshape(rows, cols)
    place = jnp.stack(
        [row_place, col_place, jnp.int32(rows_count), jnp.int32(cols_count)]
    ).astype(jnp.int32)

    panel = table[:, 0, :]
    opening = pl.pallas_call(
        open_kernel,
        out_shape=struct(pairs, mine + 2 * thin, size),
        in_specs=[SCALARS, WHOLE, WHOLE],
        compiler_params=ROOM,
        cost_estimate=cost(rows * size * size, 8 * rows * size),
    )(place, panel[: rows // 2], lax.ppermute(panel[rows // 2 :], "col", [(0, 1)]))
    found = same_core(opening)[0]
    strip = pl.pallas_call(
        strip_kernel,
        grid=(1,),
        out_shape=struct(rows_count, mine, size),
        in_specs=[SCALARS, pl.BlockSpec((size, column_blocks, size), lambda i: (0, 0, 0))],
        compiler_params=ROOM,
        cost_estimate=cost(0, 8 * size * cols),
    )(place, table)
    summed = exchange(jnp.concatenate([strip, to_all(found[mine:], rows_count)], axis=1))
    panel_chunk = summed[0, :mine]
    second_chunk = summed[1, :mine]
    square = summed[:, mine:].sum(axis=0)
    own = same_core(to_all(jnp.concatenate([found[:mine], square], axis=0), pairs))
    other = flip(own)

    images = pl.pallas_call(
        image_kernel,
        out_shape=struct(rows_count, 2 * mine, size),
        in_specs=[SCALARS, WHOLE, WHOLE, WHOLE, WHOLE],
        compiler_params=ROOM,
        cost_estimate=cost(2 * rows * cols * size, 4 * rows * (cols + 3 * size)),
    )(place, own, other, local_part, panel_chunk)
    chunks = exchange(images)
    packed = factors(own, other)

    middle = pl.pallas_call(
        middle_kernel,
        out_shape=struct(rows_count, mine + wide, size),
        in_specs=[SCALARS, WHOLE, WHOLE, WHOLE, WHOLE],
        compiler_params=ROOM,
        cost_estimate=cost(2 * mine * size * size * 5, 8 * rows * size),
    )(place, chunks, panel_chunk, second_chunk, packed)
    scaled = to_rows(middle[0, :mine], column_blocks)
    at_cols = exchange(middle)
    coupling = at_cols[:, mine:].sum(axis=0)

    part = same_core(to_all(jnp.concatenate([scaled, coupling], axis=0), pairs))
    rest = flip(part)
    coupling = (part[:, mine:] + rest[:, mine:]).sum(axis=0)
    coupling = exchange(to_all(coupling, rows_count))

    even = col_place % 2 == 0
    own_rows = own[:, :mine].reshape(rows // 2, size)
    other_rows = other[:, :mine].reshape(rows // 2, size)
    panel_rows = jnp.concatenate(
        [jnp.where(even, own_rows, other_rows), jnp.where(even, other_rows, own_rows)], axis=0
    )
    inverse = packed[2 * size : 3 * size]
    unit_lower = packed[3 * size : 4 * size]
    row_block = jnp.repeat(jnp.arange(local_blocks) * rows_count + row_place, size)
    reflect_rows = jnp.where(
        (row_block == 1)[:, None],
        jnp.tile(unit_lower, (local_blocks, 1)),
        product(panel_rows, inverse),
    )
    column_block = jnp.repeat(jnp.arange(column_blocks) * cols_count + col_place, size)
    reflect_cols = jnp.where(
        (column_block == 1)[:, None],
        jnp.tile(unit_lower, (column_blocks, 1)),
        product(chunks[:, mine:].reshape(cols, size), inverse),
    )
    banded = pl.pallas_call(
        close_kernel,
        grid=(column_blocks,),
        out_shape=struct(rows, column_blocks, size),
        in_specs=[SCALARS] + [WHOLE] * 8,
        out_specs=pl.BlockSpec((ratio * size, column_blocks, size), lambda i: (i, 0, 0)),
        scratch_shapes=[
            pltpu.VMEM((cols, 2 * size), jnp.bfloat16),
            pltpu.VMEM((cols, 2 * size), jnp.bfloat16),
        ],
        compiler_params=ROOM,
        cost_estimate=cost(4 * rows * cols * size, 8 * rows * cols),
    )(place, local_part, at_cols, reflect_cols, part, rest, coupling, reflect_rows, packed)
    return (
        banded.reshape(matrix.shape),
        reflect_rows.reshape(local_blocks, 1, size, size),
    )


def solution(mesh):
    in_specs = (P(None, "row", None, None, "col", None),)
    out_specs = (P(None, "row", None, None, "col", None), P(None, "row", None, None))
    return jax.shard_map(
        on_device, mesh=mesh, in_specs=in_specs, out_specs=out_specs, check_vma=False
    )
```

time: 198 us -> 174 us (0.88)
  blocking collectives: 31.8 us -> 16.4 us
  matrix products: 12.4 us -> 1.72 us
  Pallas kernels: 17 us -> 25.6 us
  waiting for transfers between devices: 61.9 us -> 55.4 us
  starting transfers between devices: 51 us -> 56.1 us
  local copies, waits for them, and re-layouts: 16.4 us -> 13.6 us
    all_to_all x6, waiting for transfers between devices: 61.9 us -> 46.2 us  [the longest x4 27.4 us: exchange(): return lax.all_to_all(array, 'row', 0, 0)]
    all_to_all x1, blocking collectives: 31.8 us -> 16.4 us  [same_core(): return lax.all_to_all(array, 'col', 0, 0, axis_index_groups=groups)]
    ppermute x0 -> x3, starting transfers between devices: none -> 12.2 us  [the longest x2 10.9 us: flip(): return lax.ppermute(array, 'col', [(i, i ^ 1) for i in range(count)])]
    dot_general x9 -> x2, matrix products: 12.4 us -> 1.72 us  [product(): lax.dot_general(first, second, (((first_dim,), (second_dim,)), ((), ())),...]
    ppermute x0 -> x3, waiting for transfers between devices: none -> 9.16 us  [the longest x1 7.8 us: on_device(): lax.ppermute(panel[rows // 2:], 'col', [(0, 1)])]
    pallas_call x1 -> x6, Pallas kernels: 17 us -> 25.6 us  [the longest x1 15.4 us: factors(): pl.pallas_call(functools.partial(factor_kernel, step=STEP), out_shape=str...]
    unnamed x21 -> x17, local copies, waits for them, and re-layouts: 1.85 us -> 9.34 us
    all_to_all x6, starting transfers between devices: 43.5 us -> 38.1 us  [the longest x4 27.3 us: exchange(): return lax.all_to_all(array, 'row', 0, 0)]
  transfers between devices with their start and end apart: 7 -> 10, of which waited for: 5 -> 8; matrix products, arithmetic and copies ran while one was open for 3% -> 4% of each run, Pallas kernels for 9% -> 9%
where the time goes in v2:
time: 174 us; the launch traced here: 173 us
  starting transfers between devices  56.1 us (32%)
  waiting for transfers between devices  55.4 us (32%)
  Pallas kernels  25.6 us (15%)
  blocking collectives  16.4 us (9%)
  local copies, waits for them, and re-layouts  13.6 us (8%)
  other arithmetic  3.63 us (2%)
    all_to_all x4, waiting for transfers between devices, exchange(): return lax.all_to_all(array, 'row', 0, 0)  27.4 us
    all_to_all x4, starting transfers between devices, exchange(): return lax.all_to_all(array, 'row', 0, 0)  27.3 us
    all_to_all x2, waiting for transfers between devices, same_core(): return lax.all_to_all(array, 'col', 0, 0, axis_index_groups=groups)  18.8 us
    all_to_all x1, blocking collectives, same_core(): return lax.all_to_all(array, 'col', 0, 0, axis_index_groups=groups)  16.4 us
    pallas_call x1, Pallas kernels, factors(): pl.pallas_call(functools.partial(factor_kernel, step=STEP), out_shape=str...  15.4 us
    ppermute x2, starting transfers between devices, flip(): return lax.ppermute(array, 'col', [(i, i ^ 1) for i in range(count)])  10.9 us
    all_to_all x2, starting transfers between devices, same_core(): return lax.all_to_all(array, 'col', 0, 0, axis_index_groups=groups)  10.9 us
    unnamed x17, local copies, waits for them, and re-layouts  9.34 us
  transfers between devices with their start and end apart: 10, of which 8 were waited for; matrix products, arithmetic and copies ran while one was open for 4% of the time, Pallas kernels for 9%

profile of v2, /device:TPU:1, one launch (start us, length us, event | category | flops | bytes accessed | tf_op | source)
XLA Modules:
  0.0 173.3 jit_solution(6678438162430723307)
XLA Ops:
  0.6 1.9 %fusion.9 = (f32[512,1,128]{2,1,0:T(1,128)S(1)}, f32[512,1,128]{2,1,0:T(1,128)S(1)}) fusion(f32[1024,4,128]{2,1,0:T(4,128)} %bitcast.42), kind=kLoop, calls=%fused_computation.30 | loop fusion | bytes 1048576 | tf_op jit(solution)/shard_map/slice | solution.py:345
  2.5 1.3 collective-permute-start
  3.8 0.1 pad_add_fusion.place
  3.9 7.8 %collective-permute-done.other_ref = f32[512,128]{1,0:T(8,128)S(1)} collective-permute-done((f32[512,128]{1,0:T(8,128)S(1)}, f32[512,128]{1,0:T(8,128)S(1)}, u32[]{:S(2)}, u32[]{:S(2)}) %collective-permute-start) | collective-permute-done | bytes 262176 | tf_op jit(solution)/shard_map/ppermute | solution.py:345
  11.7 1.7 shard_map.30
  13.4 3.6 %all-to-all-start = ((f32[16,48,128]{2,1,0:T(8,128)}), f32[16,48,128]{2,1,0:T(8,128)S(1)}, u32[]{:S(2)}, u32[]{:S(2)}) async-start(f32[16,48,128]{2,1,0:T(8,128)} %shard_map.30), calls=%async_computation | async-start | bytes 786432 | tf_op jit(solution)/shard_map/all_to_all | solution.py:290
  17.0 0.0 copy-start
  17.0 1.6 copy-done
  18.6 0.7 shard_map.31
  19.3 8.7 %all-to-all-done = f32[16,48,128]{2,1,0:T(8,128)S(1)} async-done(((f32[16,48,128]{2,1,0:T(8,128)}), f32[16,48,128]{2,1,0:T(8,128)S(1)}, u32[]{:S(2)}, u32[]{:S(2)}) %all-to-all-start) | async-done | bytes 393248 | tf_op jit(solution)/shard_map/all_to_all | solution.py:290
  28.0 0.8 pad_maximum_fusion
  28.8 9.0 %all-to-all-start.1 = ((f32[16,48,128]{2,1,0:T(8,128)}), f32[16,48,128]{2,1,0:T(8,128)S(1)}, u32[]{:S(2)}, u32[]{:S(2)}) async-start(f32[16,48,128]{2,1,0:T(8,128)} %pad_maximum_fusion), calls=%async_computation.1 | async-start | bytes 786432 | tf_op jit(solution)/shard_map/all_to_all | solution.py:284
  37.8 12.3 %all-to-all-done.1 = f32[16,48,128]{2,1,0:T(8,128)S(1)} async-done(((f32[16,48,128]{2,1,0:T(8,128)}), f32[16,48,128]{2,1,0:T(8,128)S(1)}, u32[]{:S(2)}, u32[]{:S(2)}) %all-to-all-start.1) | async-done | bytes 393248 | tf_op jit(solution)/shard_map/all_to_all | solution.py:284
  50.2 16.4 %all_to_all.35.own_ref = f32[16,48,128]{2,1,0:T(8,128)S(1)} all-to-all(f32[16,48,128]{2,1,0:T(8,128)S(1)} %broadcast_in_dim.52), channel_id=1, replica_groups={{0,2,4,6,8,10,12,14,16,18,20,22,24,26,28,30},{1,3,5,7,9,11,13,15,17,19,..., dimensions={0} | all-to-all | bytes 786432 | tf_op jit(solution)/shard_map/all_to_all | solution.py:290
  66.6 6.8 %collective-permute-start.1 = (f32[16,48,128]{2,1,0:T(8,128)S(1)}, f32[16,48,128]{2,1,0:T(8,128)S(1)}, u32[]{:S(2)}, u32[]{:S(2)}) collective-permute-start(f32[16,48,128]{2,1,0:T(8,128)S(1)} %all_to_all.35.own_ref), channel_id=1, source_target_pairs={{0,1},{1,0},{2,3},{3,2},{4,5},{5,4},{6,7},{7,6},{8,9},{9,8},{10,11... | collective-permute-start | bytes 1179656 | tf_op jit(solution)/shard_map/ppermute | solution.py:295
  73.4 1.8 %copy.7 = f32[128,8,4,128]{3,1,2,0:T(8,128)S(1)} copy(f32[128,8,4,128]{3,2,1,0:T(4,128)} %bitcast.43) | data formatting | bytes 4194304
  75.2 0.0 collective-permute-done.1.other_ref
  75.2 1.3 shard_map.32
  76.5 0.0 copy-start.1
  76.5 0.7 copy-done.1
  77.3 0.0 copy-start.4
  77.3 0.8 copy-done.4
  78.1 3.9 %all-to-all-start.3 = ((f32[16,64,128]{2,1,0:T(8,128)}), f32[16,64,128]{2,1,0:T(8,128)S(1)}, u32[]{:S(2)}, u32[]{:S(2)}) async-start(f32[16,64,128]{2,1,0:T(8,128)} %copy-done.4), calls=%async_computation.3 | async-start | bytes 1048576 | tf_op jit(solution)/shard_map/all_to_all | solution.py:284
  82.0 0.0 copy-start.2
  82.0 1.0 copy-done.2
  83.0 15.4 %shard_map.33.factors_ref = f32[768,128]{1,0:T(8,128)S(1)} custom-call(f32[16,48,128]{2,1,0:T(8,128)S(1)} %all_to_all.35.own_ref, f32[16,48,128]{2,1,0:T(8,128)S(1)} %copy-done.2), custom_call_target="tpu_custom_call" | custom-call | flops 268435456 | bytes 33554432 | tf_op jit(solution)/shard_map/pallas_call | solution.py:266
  98.5 1.4 all-to-all-done.3.found_ref
  99.9 1.1 shard_map.34
  101.0 0.0 copy-start.5
  101.0 0.7 copy-done.5
  101.7 7.7 %all-to-all-start.4 = ((f32[16,40,128]{2,1,0:T(8,128)}), f32[16,40,128]{2,1,0:T(8,128)}, u32[]{:S(2)}, u32[]{:S(2)}) async-start(f32[16,40,128]{2,1,0:T(8,128)} %copy-done.5), calls=%async_computation.4 | async-start | bytes 655360 | tf_op jit(solution)/shard_map/all_to_all | solution.py:284
  109.4 0.7 slice_bitcast_fusion
  110.2 5.8 %collective-permute-start.2 = (f32[32,128]{1,0:T(8,128)S(1)}, f32[32,128]{1,0:T(8,128)S(1)}, u32[]{:S(2)}, u32[]{:S(2)}) collective-permute-start(f32[32,128]{1,0:T(8,128)S(1)} %slice_bitcast_fusion), channel_id=1, source_target_pairs={{0,0},{256,1},{32,2},{288,3},{64,4},{320,5},{96,6},{352,7},{16,8},... | collective-permute-start | bytes 49160 | tf_op jit(solution)/shard_map/ppermute | solution.py:314
  116.0 7.1 %all-to-all-done.4.cols_ref = f32[16,40,128]{2,1,0:T(8,128)} async-done(((f32[16,40,128]{2,1,0:T(8,128)}), f32[16,40,128]{2,1,0:T(8,128)}, u32[]{:S(2)}, u32[]{:S(2)}) %all-to-all-start.4) | async-done | bytes 327712 | tf_op jit(solution)/shard_map/all_to_all | solution.py:284
  123.0 0.9 slice_reduce_fusion.1
  123.9 0.0 collective-permute-done.2
  123.9 0.7 broadcast_in_dim.55
  124.7 7.3 %all-to-all-start.5 = ((f32[16,40,128]{2,1,0:T(8,128)}), f32[16,40,128]{2,1,0:T(8,128)}, u32[]{:S(2)}, u32[]{:S(2)}) async-start(f32[16,40,128]{2,1,0:T(8,128)} %broadcast_in_dim.55), calls=%async_computation.5 | async-start | bytes 655360 | tf_op jit(solution)/shard_map/all_to_all | solution.py:290
  132.0 0.1 broadcast_bitcast_fusion.1
  132.1 10.1 %all-to-all-done.5.own_ref = f32[16,40,128]{2,1,0:T(8,128)} async-done(((f32[16,40,128]{2,1,0:T(8,128)}), f32[16,40,128]{2,1,0:T(8,128)}, u32[]{:S(2)}, u32[]{:S(2)}) %all-to-all-start.5) | async-done | bytes 327712 | tf_op jit(solution)/shard_map/all_to_all | solution.py:290
  142.2 4.1 %collective-permute-start.3 = (f32[16,40,128]{2,1,0:T(8,128)}, f32[16,40,128]{2,1,0:T(8,128)S(1)}, u32[]{:S(2)}, u32[]{:S(2)}) collective-permute-start(f32[16,40,128]{2,1,0:T(8,128)} %all-to-all-done.5.own_ref), channel_id=1, source_target_pairs={{0,1},{1,0},{2,3},{3,2},{4,5},{5,4},{6,7},{7,6},{8,9},{9,8},{10,11... | collective-permute-start | bytes 983048 | tf_op jit(solution)/shard_map/ppermute | solution.py:295
  146.3 0.1 broadcast_bitcast_fusion
  146.4 1.4 collective-permute-done.3.other_ref
  147.7 0.9 fusion.4
  148.6 0.0 copy-start.6
  148.6 0.7 copy-done.6
  149.4 0.6 broadcast_in_dim.56
  150.0 6.6 %all-to-all-start.6 = ((f32[16,8,128]{2,1,0:T(8,128)}), f32[16,8,128]{2,1,0:T(8,128)S(1)}, u32[]{:S(2)}, u32[]{:S(2)}) async-start(f32[16,8,128]{2,1,0:T(8,128)} %broadcast_in_dim.56), calls=%async_computation.6 | async-start | bytes 131072 | tf_op jit(solution)/shard_map/all_to_all | solution.py:284
  156.6 1.0 slice_select_fusion.1
  157.6 1.4 bitcast_select_fusion.reflect_ref
  159.0 0.4 bitcast_select_fusion.1.reflect_cols_ref
  159.4 6.6 %all-to-all-done.6.coupling_ref = f32[16,8,128]{2,1,0:T(8,128)S(1)} async-done(((f32[16,8,128]{2,1,0:T(8,128)}), f32[16,8,128]{2,1,0:T(8,128)S(1)}, u32[]{:S(2)}, u32[]{:S(2)}) %all-to-all-start.6) | async-done | bytes 65568 | tf_op jit(solution)/shard_map/all_to_all | solution.py:284
  166.0 0.0 copy-start.3
  166.0 1.0 copy-done.3
  167.0 0.0 copy-start.7
  167.0 1.0 copy-done.7
  168.0 5.3 %shard_map.35 = f32[1024,4,128]{2,1,0:T(4,128)} custom-call(s32[4]{0:T(128)S(1)} %pad_add_fusion.place, f32[1024,512]{1,0:T(8,128)S(1)} %bitcast.41, f32[16,40,128]{2,1,0:T(8,128)} %all-to-all-done.4.cols_ref, f32[512,128]{1,0:T(8,128)S(1)} %bitcast_select_fusion.1.reflect_cols_ref, f32[16,40,128]{2,1,0:T(8,128)} %all-to-all-done.5.own_ref, ...), custom_call_target="tpu_custom_call" | custom-call | flops 268435456 | bytes 4194304 | tf_op jit(solution)/shard_map/pallas_call | solution.py:408
  (12 shorter events, 0.1 us)
Async XLA Ops:
  2.5 9.2 %collective-permute-start = (f32[512,128]{1,0:T(8,128)S(1)}, f32[512,128]{1,0:T(8,128)S(1)}, u32[]{:S(2)}, u32[]{:S(2)}) collective-permute-start(f32[512,128]{1,0:T(8,128)S(1)} %bitcast.51), channel_id=1, source_target_pairs={{0,1},{32,33},{64,65},{96,97},{128,129},{160,161},{192,193},{224,2... | collective-permute-start | bytes 786440 | tf_op jit(solution)/shard_map/ppermute | solution.py:345
  13.4 14.6 %all-to-all-start = ((f32[16,48,128]{2,1,0:T(8,128)}), f32[16,48,128]{2,1,0:T(8,128)S(1)}, u32[]{:S(2)}, u32[]{:S(2)}) async-start(f32[16,48,128]{2,1,0:T(8,128)} %shard_map.30), calls=%async_computation | async-start | bytes 786432 | tf_op jit(solution)/shard_map/all_to_all | solution.py:290
  17.0 1.6 copy-start
  28.8 21.4 %all-to-all-start.1 = ((f32[16,48,128]{2,1,0:T(8,128)}), f32[16,48,128]{2,1,0:T(8,128)S(1)}, u32[]{:S(2)}, u32[]{:S(2)}) async-start(f32[16,48,128]{2,1,0:T(8,128)} %pad_maximum_fusion), calls=%async_computation.1 | async-start | bytes 786432 | tf_op jit(solution)/shard_map/all_to_all | solution.py:284
  66.6 8.6 %collective-permute-start.1 = (f32[16,48,128]{2,1,0:T(8,128)S(1)}, f32[16,48,128]{2,1,0:T(8,128)S(1)}, u32[]{:S(2)}, u32[]{:S(2)}) collective-permute-start(f32[16,48,128]{2,1,0:T(8,128)S(1)} %all_to_all.35.own_ref), channel_id=1, source_target_pairs={{0,1},{1,0},{2,3},{3,2},{4,5},{5,4},{6,7},{7,6},{8,9},{9,8},{10,11... | collective-permute-start | bytes 1179656 | tf_op jit(solution)/shard_map/ppermute | solution.py:295
  76.5 0.7 copy-start.1
  77.3 0.8 copy-start.4
  78.1 21.8 %all-to-all-start.3 = ((f32[16,64,128]{2,1,0:T(8,128)}), f32[16,64,128]{2,1,0:T(8,128)S(1)}, u32[]{:S(2)}, u32[]{:S(2)}) async-start(f32[16,64,128]{2,1,0:T(8,128)} %copy-done.4), calls=%async_computation.3 | async-start | bytes 1048576 | tf_op jit(solution)/shard_map/all_to_all | solution.py:284
  82.0 1.0 copy-start.2
  101.0 0.7 copy-start.5
  101.7 21.3 %all-to-all-start.4 = ((f32[16,40,128]{2,1,0:T(8,128)}), f32[16,40,128]{2,1,0:T(8,128)}, u32[]{:S(2)}, u32[]{:S(2)}) async-start(f32[16,40,128]{2,1,0:T(8,128)} %copy-done.5), calls=%async_computation.4 | async-start | bytes 655360 | tf_op jit(solution)/shard_map/all_to_all | solution.py:284
  110.2 13.7 %collective-permute-start.2 = (f32[32,128]{1,0:T(8,128)S(1)}, f32[32,128]{1,0:T(8,128)S(1)}, u32[]{:S(2)}, u32[]{:S(2)}) collective-permute-start(f32[32,128]{1,0:T(8,128)S(1)} %slice_bitcast_fusion), channel_id=1, source_target_pairs={{0,0},{256,1},{32,2},{288,3},{64,4},{320,5},{96,6},{352,7},{16,8},... | collective-permute-start | bytes 49160 | tf_op jit(solution)/shard_map/ppermute | solution.py:314
  124.7 17.6 %all-to-all-start.5 = ((f32[16,40,128]{2,1,0:T(8,128)}), f32[16,40,128]{2,1,0:T(8,128)}, u32[]{:S(2)}, u32[]{:S(2)}) async-start(f32[16,40,128]{2,1,0:T(8,128)} %broadcast_in_dim.55), calls=%async_computation.5 | async-start | bytes 655360 | tf_op jit(solution)/shard_map/all_to_all | solution.py:290
  142.2 5.5 %collective-permute-start.3 = (f32[16,40,128]{2,1,0:T(8,128)}, f32[16,40,128]{2,1,0:T(8,128)S(1)}, u32[]{:S(2)}, u32[]{:S(2)}) collective-permute-start(f32[16,40,128]{2,1,0:T(8,128)} %all-to-all-done.5.own_ref), channel_id=1, source_target_pairs={{0,1},{1,0},{2,3},{3,2},{4,5},{5,4},{6,7},{7,6},{8,9},{9,8},{10,11... | collective-permute-start | bytes 983048 | tf_op jit(solution)/shard_map/ppermute | solution.py:295
  148.6 0.7 copy-start.6
  150.0 16.0 %all-to-all-start.6 = ((f32[16,8,128]{2,1,0:T(8,128)}), f32[16,8,128]{2,1,0:T(8,128)S(1)}, u32[]{:S(2)}, u32[]{:S(2)}) async-start(f32[16,8,128]{2,1,0:T(8,128)} %broadcast_in_dim.56), calls=%async_computation.6 | async-start | bytes 131072 | tf_op jit(solution)/shard_map/all_to_all | solution.py:284
  166.0 1.0 copy-start.3
  167.0 1.0 copy-start.7

commit v3 on v2

v3 whole, which is shorter than its diff:
```python
import functools
import jax
import jax.numpy as jnp
from jax import lax
from jax.experimental import pallas as pl
from jax.experimental.pallas import tpu as pltpu
from jax.sharding import PartitionSpec as P

CLOSING = 2


def product(first, second, first_dim=1, second_dim=0):
    return lax.dot_general(
        first,
        second,
        (((first_dim,), (second_dim,)), ((), ())),
        precision=lax.Precision.HIGHEST,
        preferred_element_type=jnp.float32,
    )


def halves(array):
    high = array.astype(jnp.bfloat16)
    return high, (array - high.astype(jnp.float32)).astype(jnp.bfloat16)


def passes(first, second, first_dim=1, second_dim=0):
    dims = (((first_dim,), (second_dim,)), ((), ()))

    def one(a, b):
        return lax.dot_general(a, b, dims, preferred_element_type=jnp.float32)

    return one(first[0], second[0]) + (one(first[0], second[1]) + one(first[1], second[0]))


def factor_kernel(base_ref, out_ref):
    size = base_ref.shape[1]
    lane = lax.broadcasted_iota(jnp.int32, (1, size), 1)
    lane2 = lax.broadcasted_iota(jnp.int32, (1, 2 * size), 1)
    place = lax.broadcasted_iota(jnp.int32, (size, 1), 0)
    eye = (lane == place).astype(jnp.float32)
    g = jnp.concatenate([base_ref[:size], eye], axis=1)
    w = base_ref[size:]
    e = eye
    m = eye
    band = jnp.zeros((size, size), jnp.float32)
    turned = jnp.zeros((size, size), jnp.float32)
    for i in range(size):
        below = place > i
        here = place == i
        pivot = g[i : i + 1, i : i + 1]
        root = lax.rsqrt(pivot)
        root = root * (1.5 - 0.5 * pivot * root * root)
        row = jnp.where(lane2 >= i, g[i : i + 1, :] * root, 0.0)
        g = g - jnp.where(below, g[:, i : i + 1] * root, 0.0) * row
        r_row = row[:, :size]
        w_pivot = w[i : i + 1, i : i + 1]
        sign = jnp.where(w_pivot >= 0.0, -1.0, 1.0)
        inverse = 1.0 / (w_pivot - sign * (pivot * root))
        s_row = sign * r_row
        t_row = jnp.where(lane >= i, w[i : i + 1, :], 0.0) - s_row
        l = jnp.where(below, w[:, i : i + 1] * inverse, 0.0)
        w = w - jnp.where(here, s_row, l * t_row)
        w = jnp.where((lane == i) & below, l, w)
        e = e - l * e[i : i + 1, :]
        band = jnp.where(here, s_row, band)
        turned = jnp.where(here, sign * row[:, size:], turned)
        m_column = m[:, i : i + 1] * inverse
        m = jnp.where(lane == i, m_column, m - m_column * t_row)
    upper = jnp.where(lane >= place, w, 0.0)
    triangle = -product(upper, product(e, turned), 1, 1)
    out_ref[:size] = product(m, triangle)
    out_ref[size : 2 * size] = -product(product(band, m), triangle)
    out_ref[2 * size : 3 * size] = m
    out_ref[3 * size : 4 * size] = jnp.where(place > lane, w, 0.0) + eye
    out_ref[4 * size : 5 * size] = triangle
    out_ref[5 * size :] = band


def open_kernel(place, own_ref, other_ref, out_ref):
    size = own_ref.shape[1]
    count, extent, _ = out_ref.shape
    thin = size // count
    mine = extent - 2 * thin
    core = place[1]
    panel = jnp.where(core == 0, own_ref[...], other_ref[...])
    second = jnp.where((place[0] == 1) & (core == 0), panel[:size], 0.0)
    index = lax.broadcasted_iota(jnp.int32, panel.shape, 0)
    panel = jnp.where((index < size) & (place[0] == 0) & (core == 0), 0.0, panel)
    out_ref[:, :mine, :] = panel.reshape(count, mine, size)
    out_ref[:, mine : mine + thin, :] = product(panel, panel, 0, 0).reshape(count, thin, size)
    out_ref[:, mine + thin :, :] = second.reshape(count, thin, size)


def strip_kernel(place, matrix_ref, table_ref, out_ref):
    size = matrix_ref.shape[2]
    blocks = matrix_ref.shape[1]
    count, mine, _ = out_ref.shape
    each = size // mine
    for b in range(blocks):
        table_ref[:, b * size : (b + 1) * size] = matrix_ref[:, b, :]

    @pl.when(pl.program_id(0) == 0)
    def _():
        for b in range(blocks):
            turned = matrix_ref[:size, b, :].T
            if b == 0:
                turned = jnp.where(place[1] == 0, 0.0, turned)
            out_ref[b * each : (b + 1) * each] = turned.reshape(each, mine, size)


def image_kernel(
    place, own_ref, other_ref, matrix_ref, chunk_ref, out_ref, panel_ref, base_ref
):
    size = own_ref.shape[2]
    count, extent, _ = out_ref.shape
    mine = extent // 2
    each = size // mine
    own = own_ref[:, :mine, :].reshape(-1, size)
    other = other_ref[:, :mine, :].reshape(-1, size)
    even = place[1] % 2 == 0
    panel = jnp.concatenate([jnp.where(even, own, other), jnp.where(even, other, own)], axis=0)
    panel_ref[...] = panel
    both = own_ref[:, mine:, :] + other_ref[:, mine:, :]
    thin = both.shape[1] // 2
    base_ref[:size] = both[:, :thin].reshape(size, size)
    base_ref[size:] = both[:, thin:].reshape(size, size)
    high, low = halves(panel.T)
    matrix_high, matrix_low = halves(matrix_ref[...])
    image = jnp.dot(
        jnp.concatenate([high, low], axis=0), matrix_high, preferred_element_type=jnp.float32
    )
    image = image[:size] + (
        image[size:] + jnp.dot(high, matrix_low, preferred_element_type=jnp.float32)
    )
    for b in range(matrix_ref.shape[1] // size):
        turned = image[:, b * size : (b + 1) * size].T
        out_ref[b * each : (b + 1) * each, :mine, :] = turned.reshape(each, mine, size)
    out_ref[:, mine:, :] = jnp.broadcast_to(chunk_ref[...][None], (count, mine, size))


def middle_kernel(place, found_ref, panel_ref, second_ref, factors_ref, out_ref, scaled_ref):
    size = factors_ref.shape[1]
    count, extent, _ = found_ref.shape
    mine = extent // 2
    wide = size // count
    image = found_ref[0, :mine, :]
    for p in range(1, count):
        image = image + found_ref[p, :mine, :]
    block = (place[0] * mine) // size * place[3] + place[1]
    both = jnp.concatenate([image, second_ref[...]], axis=1)
    scaled = product(both, factors_ref[: 2 * size])
    scaled = jnp.where(block == 0, 0.0, scaled)
    reflect = product(panel_ref[...], factors_ref[2 * size : 3 * size])
    offset = pl.multiple_of(3 * size + (place[0] * mine) % size, mine)
    reflect = jnp.where(block == 1, factors_ref[pl.ds(offset, mine), :], reflect)
    reflect = jnp.where(block == 0, 0.0, reflect)
    coupling = product(reflect, scaled, 0, 0)
    scaled_ref[...] = scaled
    out_ref[:, :mine, :] = jnp.broadcast_to(scaled[None], (count, mine, size))
    out_ref[:, mine:, :] = coupling.reshape(count, wide, size)


def gather_kernel(found_ref, other_ref, scaled_ref, out_ref):
    mine = scaled_ref.shape[0]
    count = out_ref.shape[0]
    out_ref[:, :mine, :] = jnp.broadcast_to(scaled_ref[...][None], (count,) + scaled_ref.shape)
    pieces = found_ref[:, mine:, :].sum(axis=0) + other_ref[...]
    out_ref[:, mine:, :] = jnp.broadcast_to(pieces[None], (count,) + pieces.shape)


def coupling_kernel(part_ref, out_ref, scaled_ref):
    mine = scaled_ref.shape[1]
    pieces = part_ref[:, mine:, :].sum(axis=0)
    out_ref[...] = jnp.broadcast_to(pieces[None], out_ref.shape)
    scaled_ref[...] = part_ref[:, :mine, :]


def reflect_kernel(place, panel_ref, chunks_ref, factors_ref, ready_ref, rows_ref, cols_ref):
    del ready_ref
    size = factors_ref.shape[1]
    mine = chunks_ref.shape[1] // 2
    inverse = factors_ref[2 * size : 3 * size]
    unit_lower = factors_ref[3 * size : 4 * size]
    rows_ref[...] = product(panel_ref[...], inverse)
    cols_ref[...] = product(chunks_ref[:, mine:, :].reshape(-1, size), inverse)

    @pl.when(place[0] == 1)
    def _():
        rows_ref[:size] = unit_lower

    @pl.when(place[1] == 1)
    def _():
        cols_ref[:size] = unit_lower


def close_kernel(
    place,
    matrix_ref,
    cols_ref,
    reflect_cols_ref,
    own_ref,
    other_ref,
    coupling_ref,
    reflect_ref,
    triangle_ref,
    band_ref,
    out_ref,
    high,
    low,
):
    step = pl.program_id(0)
    size = band_ref.shape[1]
    mine = own_ref.shape[1]
    blocks = out_ref.shape[1]
    extent = out_ref.shape[0]
    parts = size // mine
    pairs, count = own_ref.shape[0], cols_ref.shape[0]
    ratio = 2 * pairs // count

    @pl.when(step == 0)
    def _():
        coupling = coupling_ref[...].reshape(size, size)
        correction = product(triangle_ref[...], coupling, 0, 0)
        reflect_cols = reflect_cols_ref[...]
        scaled_cols = cols_ref[:, :mine, :].reshape(-1, size)
        update = scaled_cols - passes(halves(reflect_cols), halves(correction))
        right = halves(jnp.concatenate([update, reflect_cols], axis=1))
        high[...] = right[0]
        low[...] = right[1]

    scaled = []
    for k in range(extent // mine):
        block, part = divmod(k, parts)
        source = (step * (extent // size // ratio) + block // ratio) * parts + part
        col = block % ratio * count + lax.rem(source + count // 2, count)
        here = lax.rem(col, 2) == lax.rem(place[1], 2)
        at = lax.div(col, 2)
        scaled.append(jnp.where(here, own_ref[at], other_ref[at]))
    left = jnp.concatenate([reflect_ref[...], jnp.concatenate(scaled, axis=0)], axis=1)
    value = matrix_ref[...] - passes(halves(left), (high[...], low[...]), 1, 1)
    band = band_ref[...]
    for h in range(extent // size):
        row_block = (step * (extent // size) + h) * place[2] + place[0]
        for b in range(blocks):
            column_block = b * place[3] + place[1]
            tile = value[h * size : (h + 1) * size, b * size : (b + 1) * size]
            if b == 0:
                rim = jnp.where(row_block == 1, band, 0.0)
                tile = jnp.where((column_block == 0) & (row_block >= 1), rim, tile)
            if h == 0:
                rim = jnp.where(column_block == 1, band.T, 0.0) if b == 0 else jnp.zeros_like(band)
                tile = jnp.where((row_block == 0) & (column_block >= 1), rim, tile)
            out_ref[h * size : (h + 1) * size, b, :] = tile


def cost(flops, moved):
    return pl.CostEstimate(flops=flops, bytes_accessed=moved, transcendentals=0)


def struct(*shape):
    return jax.ShapeDtypeStruct(shape, jnp.float32)


SCALARS = pl.BlockSpec(memory_space=pltpu.SMEM)
WHOLE = pl.BlockSpec(memory_space=pltpu.VMEM)


def entire(array):
    return pl.BlockSpec(array.shape, lambda i: (0,) * array.ndim)


ROOM = pltpu.CompilerParams(vmem_limit_bytes=24 << 20)
MORE = pltpu.CompilerParams(vmem_limit_bytes=56 << 20)


def factors(base):
    size = base.shape[1]
    return pl.pallas_call(
        factor_kernel,
        out_shape=struct(6 * size, size),
        compiler_params=ROOM,
        cost_estimate=cost(1 << 28, 1 << 25),
    )(base)


def exchange(array):
    return lax.all_to_all(array, "row", 0, 0)


def same_core(array):
    count = lax.axis_size("col")
    groups = [list(range(core, count, 2)) for core in range(2)]
    return lax.all_to_all(array, "col", 0, 0, axis_index_groups=groups)


def flip(array):
    count = lax.axis_size("col")
    return lax.ppermute(array, "col", [(i, i ^ 1) for i in range(count)])


def to_all(array, count):
    return jnp.broadcast_to(array[None], (count,) + array.shape)


def to_rows(chunk):
    rows_count = lax.axis_size("row")
    cols_count = lax.axis_size("col")
    pairs = []
    for row in range(rows_count):
        for col in range(cols_count):
            half, k = divmod(col, rows_count)
            source = (k + rows_count // 2) % rows_count * cols_count + half * rows_count + row
            pairs.append((source, row * cols_count + col))
    return lax.ppermute(chunk, ("row", "col"), pairs)


def on_device(matrix):
    rows_count = lax.axis_size("row")
    cols_count = lax.axis_size("col")
    row_place = lax.axis_index("row")
    col_place = lax.axis_index("col")
    local_blocks = matrix.shape[0]
    size = matrix.shape[2]
    column_blocks = matrix.shape[3]
    rows = local_blocks * size
    cols = column_blocks * size
    ratio = cols_count // rows_count
    pairs = cols_count // 2
    mine = rows // cols_count
    thin = size // pairs
    wide = size // rows_count
    table = matrix.reshape(rows, column_blocks, size)
    place = jnp.stack(
        [row_place, col_place, jnp.int32(rows_count), jnp.int32(cols_count)]
    ).astype(jnp.int32)

    panel = table[:, 0, :]
    opening = pl.pallas_call(
        open_kernel,
        out_shape=struct(pairs, mine + 2 * thin, size),
        in_specs=[SCALARS, WHOLE, WHOLE],
        compiler_params=ROOM,
        cost_estimate=cost(rows * size * size, 8 * rows * size),
    )(place, panel[: rows // 2], lax.ppermute(panel[rows // 2 :], "col", [(0, 1)]))
    found = same_core(opening)[0]
    local_part, strip = pl.pallas_call(
        strip_kernel,
        grid=(column_blocks,),
        out_shape=(struct(rows, cols), struct(rows_count, mine, size)),
        in_specs=[
            SCALARS,
            pl.BlockSpec((rows // column_blocks, column_blocks, size), lambda i: (i, 0, 0)),
        ],
        out_specs=(
            pl.BlockSpec((rows // column_blocks, cols), lambda i: (i, 0)),
            pl.BlockSpec((rows_count, mine, size), lambda i: (0, 0, 0)),
        ),
        compiler_params=ROOM,
        cost_estimate=cost(0, 8 * rows * cols),
    )(place, table)
    summed = exchange(jnp.concatenate([strip, to_all(found[mine:], rows_count)], axis=1))
    panel_chunk = summed[0, :mine]
    second_chunk = summed[1, :mine]
    square = summed[:, mine:].sum(axis=0)
    own = same_core(to_all(jnp.concatenate([found[:mine], square], axis=0), pairs))
    other = flip(own)

    images, panel_rows, base = pl.pallas_call(
        image_kernel,
        out_shape=(struct(rows_count, 2 * mine, size), struct(rows, size), struct(2 * size, size)),
        in_specs=[SCALARS, WHOLE, WHOLE, WHOLE, WHOLE],
        compiler_params=ROOM,
        cost_estimate=cost(2 * rows * cols * size, 4 * rows * (cols + 3 * size)),
    )(place, own, other, local_part, panel_chunk)
    chunks = exchange(images)
    packed = factors(base)

    middle, scaled = pl.pallas_call(
        middle_kernel,
        out_shape=(struct(rows_count, mine + wide, size), struct(mine, size)),
        in_specs=[SCALARS, WHOLE, WHOLE, WHOLE, WHOLE],
        compiler_params=ROOM,
        cost_estimate=cost(2 * mine * size * size * 5, 8 * rows * size),
    )(place, chunks, panel_chunk, second_chunk, packed)
    scaled = to_rows(scaled)
    at_cols = exchange(middle)

    gathering = pl.pallas_call(
        gather_kernel,
        out_shape=struct(pairs, mine + wide, size),
        compiler_params=ROOM,
        cost_estimate=cost(0, 4 * rows * size),
    )(at_cols, flip(at_cols[:, mine:].sum(axis=0)), scaled)
    part = same_core(gathering)
    coupling, part = pl.pallas_call(
        coupling_kernel,
        out_shape=(struct(rows_count, wide, size), struct(pairs, mine, size)),
        compiler_params=ROOM,
        cost_estimate=cost(0, 4 * rows * size),
    )(part)
    reflect_rows, reflect_cols = pl.pallas_call(
        reflect_kernel,
        out_shape=(struct(rows, size), struct(cols, size)),
        in_specs=[SCALARS, WHOLE, WHOLE, WHOLE, pl.BlockSpec(memory_space=pl.ANY)],
        compiler_params=ROOM,
        cost_estimate=cost(4 * rows * size * size, 8 * rows * size),
    )(place, panel_rows, chunks, packed, coupling)
    coupling = exchange(coupling)
    rest = flip(part)
    extent = ratio * size * max(1, column_blocks // CLOSING)
    banded = pl.pallas_call(
        close_kernel,
        grid=(rows // extent,),
        out_shape=struct(rows, column_blocks, size),
        in_specs=[
            SCALARS,
            pl.BlockSpec((extent, cols), lambda i: (i, 0)),
            entire(at_cols),
            entire(reflect_cols),
            entire(part),
            entire(rest),
            entire(coupling),
            pl.BlockSpec((extent, size), lambda i: (i, 0)),
            pl.BlockSpec((size, size), lambda i: (4, 0)),
            pl.BlockSpec((size, size), lambda i: (5, 0)),
        ],
        out_specs=pl.BlockSpec((extent, column_blocks, size), lambda i: (i, 0, 0)),
        scratch_shapes=[
            pltpu.VMEM((cols, 2 * size), jnp.bfloat16),
            pltpu.VMEM((cols, 2 * size), jnp.bfloat16),
        ],
        compiler_params=MORE,
        cost_estimate=cost(4 * rows * cols * size, 8 * rows * cols),
    )(place, local_part, at_cols, reflect_cols, part, rest, coupling, reflect_rows, packed, packed)
    return (
        banded.reshape(matrix.shape),
        reflect_rows.reshape(local_blocks, 1, size, size),
    )


def solution(mesh):
    in_specs = (P(None, "row", None, None, "col", None),)
    out_specs = (P(None, "row", None, None, "col", None), P(None, "row", None, None))
    return jax.shard_map(
        on_device, mesh=mesh, in_specs=in_specs, out_specs=out_specs, check_vma=False
    )
```

time: 174 us -> 164 us (0.943)
  blocking collectives: 16.4 us -> 31.1 us
  waiting for transfers between devices: 55.4 us -> 45.3 us
  local copies, waits for them, and re-layouts: 13.6 us -> 4.69 us
  starting transfers between devices: 56.1 us -> 50.8 us
  Pallas kernels: 25.6 us -> 29.4 us
  other arithmetic: 3.63 us -> 0.89 us
    all_to_all x1 -> x2, blocking collectives: 16.4 us -> 31.1 us  [same_core(): return lax.all_to_all(array, 'col', 0, 0, axis_index_groups=groups)]
    all_to_all x2 -> x1, waiting for transfers between devices: 18.8 us -> 7.7 us  [same_core(): return lax.all_to_all(array, 'col', 0, 0, axis_index_groups=groups)]
    all_to_all x2 -> x1, starting transfers between devices: 10.9 us -> 3.55 us  [same_core(): return lax.all_to_all(array, 'col', 0, 0, axis_index_groups=groups)]
    unnamed x17, local copies, waits for them, and re-layouts: 9.34 us -> 3.26 us
    all_to_all x4, starting transfers between devices: 27.3 us -> 21.5 us  [exchange(): return lax.all_to_all(array, 'row', 0, 0)]
    ppermute x2 -> x3, starting transfers between devices: 10.9 us -> 16.3 us  [flip(): return lax.ppermute(array, 'col', [(i, i ^ 1) for i in range(count)])]
    pallas_call x5 -> x8, Pallas kernels: 23.9 us -> 27.7 us  [the longest x1 13.5 us: factors(): pl.pallas_call(factor_kernel, out_shape=struct(6 * size, size), compiler_...]
    ppermute x1, starting transfers between devices: 5.77 us -> 8.13 us  [to_rows(): return lax.ppermute(chunk, ('row', 'col'), pairs)]
  transfers between devices with their start and end apart: 10 -> 10, of which waited for: 8 -> 8; matrix products, arithmetic and copies ran while one was open for 4% -> 1% of each run, Pallas kernels for 9% -> 11%
where the time goes in v3:
time: 164 us; the launch traced here: 163 us
  starting transfers between devices  50.8 us (31%)
  waiting for transfers between devices  45.3 us (28%)
  blocking collectives  31.1 us (19%)
  Pallas kernels  29.4 us (18%)
  local copies, waits for them, and re-layouts  4.69 us (3%)
    all_to_all x2, blocking collectives, same_core(): return lax.all_to_all(array, 'col', 0, 0, axis_index_groups=groups)  31.1 us
    all_to_all x4, waiting for transfers between devices, exchange(): return lax.all_to_all(array, 'row', 0, 0)  27.7 us
    all_to_all x4, starting transfers between devices, exchange(): return lax.all_to_all(array, 'row', 0, 0)  21.5 us
    ppermute x3, starting transfers between devices, flip(): return lax.ppermute(array, 'col', [(i, i ^ 1) for i in range(count)])  16.3 us
    pallas_call x1, Pallas kernels, factors(): pl.pallas_call(factor_kernel, out_shape=struct(6 * size, size), compiler_...  13.5 us
    ppermute x1, starting transfers between devices, to_rows(): return lax.ppermute(chunk, ('row', 'col'), pairs)  8.13 us
    ppermute x1, waiting for transfers between devices, on_device(): lax.ppermute(panel[rows // 2:], 'col', [(0, 1)])  7.8 us
    all_to_all x1, waiting for transfers between devices, same_core(): return lax.all_to_all(array, 'col', 0, 0, axis_index_groups=groups)  7.7 us
  transfers between devices with their start and end apart: 10, of which 8 were waited for; matrix products, arithmetic and copies ran while one was open for 1% of the time, Pallas kernels for 11%

profile of v3, /device:TPU:1, one launch (start us, length us, event | category | flops | bytes accessed | tf_op | source)
XLA Modules:
  0.0 163.1 jit_solution(4271495078308128219)
XLA Ops:
  0.6 1.8 %copy.3 = f32[8,1,128,4,1,128]{5,2,0,3,4,1:T(8,128)S(1)} copy(f32[8,1,128,4,1,128]{5,4,3,2,1,0:T(1,128)} %param.1) | data formatting | bytes 4194304 | tf_op args[0]
  2.5 1.3 collective-permute-start
  3.8 0.1 pad_add_fusion.place
  3.9 0.0 copy-start.5
  3.9 7.8 %collective-permute-done.other_ref = f32[512,128]{1,0:T(8,128)S(1)} collective-permute-done((f32[512,128]{1,0:T(8,128)S(1)}, f32[512,128]{1,0:T(8,128)S(1)}, u32[]{:S(2)}, u32[]{:S(2)}) %collective-permute-start) | collective-permute-done | bytes 262176 | tf_op jit(solution)/shard_map/ppermute | solution.py:345
  11.7 1.7 %shard_map.31 = f32[16,48,128]{2,1,0:T(8,128)} custom-call(s32[4]{0:T(128)S(1)} %pad_add_fusion.place, f32[512,128]{1,0:T(8,128)S(1)} %get-tuple-element.27.own_ref, f32[512,128]{1,0:T(8,128)S(1)} %collective-permute-done.other_ref), custom_call_target="tpu_custom_call" | custom-call | flops 16777216 | bytes 1048576 | tf_op jit(solution)/shard_map/pallas_call | solution.py:339
  13.4 3.6 %all-to-all-start = ((f32[16,48,128]{2,1,0:T(8,128)}), f32[16,48,128]{2,1,0:T(8,128)S(1)}, u32[]{:S(2)}, u32[]{:S(2)}) async-start(f32[16,48,128]{2,1,0:T(8,128)} %shard_map.31), calls=%async_computation | async-start | bytes 786432 | tf_op jit(solution)/shard_map/all_to_all | solution.py:294
  17.0 1.4 copy.4.matrix_ref
  18.3 1.9 %shard_map.30 = (f32[1024,512]{1,0:T(8,128)S(1)}, f32[16,32,128]{2,1,0:T(8,128)S(1)}) custom-call(s32[4]{0:T(128)S(1)} %pad_add_fusion.place, f32[1024,4,128]{2,1,0:T(4,128)S(1)} %copy.4.matrix_ref), custom_call_target="tpu_custom_call" | custom-call | bytes 4194304 | tf_op jit(solution)/shard_map/pallas_call | solution.py:347
  20.3 0.0 copy-start
  20.3 7.7 %all-to-all-done = f32[16,48,128]{2,1,0:T(8,128)S(1)} async-done(((f32[16,48,128]{2,1,0:T(8,128)}), f32[16,48,128]{2,1,0:T(8,128)S(1)}, u32[]{:S(2)}, u32[]{:S(2)}) %all-to-all-start) | async-done | bytes 393248 | tf_op jit(solution)/shard_map/all_to_all | solution.py:294
  28.0 0.8 pad_maximum_fusion
  28.8 9.0 %all-to-all-start.1 = ((f32[16,48,128]{2,1,0:T(8,128)}), f32[16,48,128]{2,1,0:T(8,128)S(1)}, u32[]{:S(2)}, u32[]{:S(2)}) async-start(f32[16,48,128]{2,1,0:T(8,128)} %pad_maximum_fusion), calls=%async_computation.1 | async-start | bytes 786432 | tf_op jit(solution)/shard_map/all_to_all | solution.py:288
  37.8 12.3 %all-to-all-done.1 = f32[16,48,128]{2,1,0:T(8,128)S(1)} async-done(((f32[16,48,128]{2,1,0:T(8,128)}), f32[16,48,128]{2,1,0:T(8,128)S(1)}, u32[]{:S(2)}, u32[]{:S(2)}) %all-to-all-start.1) | async-done | bytes 393248 | tf_op jit(solution)/shard_map/all_to_all | solution.py:288
  50.2 16.4 %all_to_all.35.own_ref = f32[16,48,128]{2,1,0:T(8,128)S(1)} all-to-all(f32[16,48,128]{2,1,0:T(8,128)S(1)} %broadcast_in_dim.16), channel_id=1, replica_groups={{0,2,4,6,8,10,12,14,16,18,20,22,24,26,28,30},{1,3,5,7,9,11,13,15,17,19,..., dimensions={0} | all-to-all | bytes 786432 | tf_op jit(solution)/shard_map/all_to_all | solution.py:294
  66.6 6.8 %collective-permute-start.1 = (f32[16,48,128]{2,1,0:T(8,128)S(1)}, f32[16,48,128]{2,1,0:T(8,128)S(1)}, u32[]{:S(2)}, u32[]{:S(2)}) collective-permute-start(f32[16,48,128]{2,1,0:T(8,128)S(1)} %all_to_all.35.own_ref), channel_id=1, source_target_pairs={{0,1},{1,0},{2,3},{3,2},{4,5},{5,4},{6,7},{7,6},{8,9},{9,8},{10,11... | collective-permute-start | bytes 1179656 | tf_op jit(solution)/shard_map/ppermute | solution.py:299
  73.4 1.3 collective-permute-done.1.other_ref
  74.7 2.2 %shard_map.32 = (f32[16,64,128]{2,1,0:T(8,128)}, f32[1024,128]{1,0:T(8,128)S(1)}, f32[256,128]{1,0:T(8,128)S(1)}) custom-call(s32[4]{0:T(128)S(1)} %pad_add_fusion.place, f32[16,48,128]{2,1,0:T(8,128)S(1)} %all_to_all.35.own_ref, f32[16,48,128]{2,1,0:T(8,128)S(1)} %collective-permute-done.1.other_ref, f32[1024,512]{1,0:T(8,128)S(1)} %get-tuple-element.13.matrix_ref, ...), custom_call_target="tpu_custom_call" | custom-call | flops 134217728 | bytes 3670016 | tf_op jit(solution)/shard_map/pallas_call | solution.py:369
  76.9 0.0 copy-done
  76.9 3.9 %all-to-all-start.3 = ((f32[16,64,128]{2,1,0:T(8,128)}), f32[16,64,128]{2,1,0:T(8,128)S(1)}, u32[]{:S(2)}, u32[]{:S(2)}) async-start(f32[16,64,128]{2,1,0:T(8,128)} %get-tuple-element.15), calls=%async_computation.3 | async-start | bytes 1048576 | tf_op jit(solution)/shard_map/all_to_all | solution.py:288
  80.8 13.5 %shard_map.33.factors_ref.triangle_ref.band_ref = f32[768,128]{1,0:T(8,128)S(1)} custom-call(f32[256,128]{1,0:T(8,128)S(1)} %get-tuple-element.16.base_ref), custom_call_target="tpu_custom_call" | custom-call | flops 268435456 | bytes 33554432 | tf_op jit(solution)/shard_map/pallas_call | solution.py:279
  94.3 0.0 copy-start.1
  94.3 4.0 %all-to-all-done.3.found_ref.chunks_ref = f32[16,64,128]{2,1,0:T(8,128)S(1)} async-done(((f32[16,64,128]{2,1,0:T(8,128)}), f32[16,64,128]{2,1,0:T(8,128)S(1)}, u32[]{:S(2)}, u32[]{:S(2)}) %all-to-all-start.3) | async-done | bytes 524320 | tf_op jit(solution)/shard_map/all_to_all | solution.py:288
  98.3 1.9 %shard_map.34 = (f32[16,40,128]{2,1,0:T(8,128)}, f32[32,128]{1,0:T(8,128)S(1)}) custom-call(s32[4]{0:T(128)S(1)} %pad_add_fusion.place, f32[16,64,128]{2,1,0:T(8,128)S(1)} %all-to-all-done.3.found_ref.chunks_ref, f32[32,128]{1,0:T(8,128)S(1)} %get-tuple-element.29.chunk_ref.panel_ref, f32[32,128]{1,0:T(8,128)S(1)} %get-tuple-element.28.second_ref, ...), custom_call_target="tpu_custom_call" | custom-call | flops 5242880 | bytes 1048576 | tf_op jit(solution)/shard_map/pallas_call | solution.py:379
  100.2 5.0 %all-to-all-start.4 = ((f32[16,40,128]{2,1,0:T(8,128)}), f32[16,40,128]{2,1,0:T(8,128)S(1)}, u32[]{:S(2)}, u32[]{:S(2)}) async-start(f32[16,40,128]{2,1,0:T(8,128)} %get-tuple-element.17), calls=%async_computation.4 | async-start | bytes 655360 | tf_op jit(solution)/shard_map/all_to_all | solution.py:288
  105.3 8.1 %collective-permute-start.3 = (f32[32,128]{1,0:T(8,128)S(1)}, f32[32,128]{1,0:T(8,128)S(1)}, u32[]{:S(2)}, u32[]{:S(2)}) collective-permute-start(f32[32,128]{1,0:T(8,128)S(1)} %get-tuple-element.19), channel_id=1, source_target_pairs={{256,0},{288,1},{320,2},{352,3},{384,4},{416,5},{448,6},{480,7},{0... | collective-permute-start | bytes 49160 | tf_op jit(solution)/shard_map/ppermute | solution.py:315
  113.4 4.7 %all-to-all-done.4.found_ref.cols_ref = f32[16,40,128]{2,1,0:T(8,128)S(1)} async-done(((f32[16,40,128]{2,1,0:T(8,128)}), f32[16,40,128]{2,1,0:T(8,128)S(1)}, u32[]{:S(2)}, u32[]{:S(2)}) %all-to-all-start.4) | async-done | bytes 327712 | tf_op jit(solution)/shard_map/all_to_all | solution.py:288
  118.1 0.0 copy-start.2
  118.2 5.5 %collective-permute-start.2 = (f32[8,128]{1,0:T(8,128)S(1)}, f32[8,128]{1,0:T(8,128)S(1)}, u32[]{:S(2)}, u32[]{:S(2)}) collective-permute-start(f32[8,128]{1,0:T(8,128)S(1)} %slice_reduce_fusion.1), channel_id=1, source_target_pairs={{0,1},{1,0},{2,3},{3,2},{4,5},{5,4},{6,7},{7,6},{8,9},{9,8},{10,11... | collective-permute-start | bytes 12296 | tf_op jit(solution)/shard_map/ppermute | solution.py:299
  123.7 0.0 collective-permute-done.3.scaled_ref
  123.7 0.8 collective-permute-done.2.other_ref
  124.5 14.8 %all_to_all.36.part_ref = f32[16,40,128]{2,1,0:T(8,128)S(1)} all-to-all(f32[16,40,128]{2,1,0:T(8,128)S(1)} %shard_map.35), channel_id=1, replica_groups={{0,2,4,6,8,10,12,14,16,18,20,22,24,26,28,30},{1,3,5,7,9,11,13,15,17,19,..., dimensions={0} | all-to-all | bytes 655360 | tf_op jit(solution)/shard_map/all_to_all | solution.py:294
  139.3 0.7 shard_map.36
  139.9 0.0 copy-start.3
  139.9 4.0 %collective-permute-start.4 = (f32[16,32,128]{2,1,0:T(8,128)S(1)}, f32[16,32,128]{2,1,0:T(8,128)S(1)}, u32[]{:S(2)}, u32[]{:S(2)}) collective-permute-start(f32[16,32,128]{2,1,0:T(8,128)S(1)} %get-tuple-element.22.own_ref), channel_id=1, source_target_pairs={{0,1},{1,0},{2,3},{3,2},{4,5},{5,4},{6,7},{7,6},{8,9},{9,8},{10,11... | collective-permute-start | bytes 786440 | tf_op jit(solution)/shard_map/ppermute | solution.py:299
  144.0 3.5 %all-to-all-start.6 = ((f32[16,8,128]{2,1,0:T(8,128)}), f32[16,8,128]{2,1,0:T(8,128)S(1)}, u32[]{:S(2)}, u32[]{:S(2)}) async-start(f32[16,8,128]{2,1,0:T(8,128)} %get-tuple-element.20.ready_ref), calls=%async_computation.6 | async-start | bytes 131072 | tf_op jit(solution)/shard_map/all_to_all | solution.py:288
  147.5 0.0 copy-done.5
  147.5 2.1 %shard_map.37 = (f32[1024,128]{1,0:T(8,128)}, f32[512,128]{1,0:T(8,128)S(1)}) custom-call(s32[4]{0:T(128)S(1)} %pad_add_fusion.place, f32[1024,128]{1,0:T(8,128)S(1)} %get-tuple-element.18.panel_ref, f32[16,64,128]{2,1,0:T(8,128)S(1)} %all-to-all-done.3.found_ref.chunks_ref, f32[768,128]{1,0:T(8,128)S(1)} %shard_map.33.factors_ref.triangle_ref.band_ref, ...), custom_call_target="tpu_custom_call" | custom-call | flops 67108864 | bytes 1048576 | tf_op jit(solution)/shard_map/pallas_call | solution.py:402
  149.6 0.0 copy-done.1
  149.6 0.0 copy-start.4
  149.6 0.7 copy-done.4
  150.3 6.6 %all-to-all-done.6.coupling_ref = f32[16,8,128]{2,1,0:T(8,128)S(1)} async-done(((f32[16,8,128]{2,1,0:T(8,128)}), f32[16,8,128]{2,1,0:T(8,128)S(1)}, u32[]{:S(2)}, u32[]{:S(2)}) %all-to-all-start.6) | async-done | bytes 65568 | tf_op jit(solution)/shard_map/all_to_all | solution.py:288
  156.9 0.0 copy-start.6
  156.9 0.0 collective-permute-done.4.other_ref
  157.0 0.0 copy-start.7
  157.0 0.0 copy-done.2
  157.0 0.0 copy-done.3
  157.0 0.6 copy-done.6
  157.6 0.1 copy-done.7
  157.7 5.5 %shard_map.38 = f32[1024,4,128]{2,1,0:T(4,128)} custom-call(s32[4]{0:T(128)} %copy-done.5, f32[1024,512]{1,0:T(8,128)} %copy-done, f32[16,40,128]{2,1,0:T(8,128)} %copy-done.2, f32[512,128]{1,0:T(8,128)} %copy-done.4, f32[16,32,128]{2,1,0:T(8,128)} %copy-done.3, f32[16,32,128]{2,1,0:T(8,128)} %copy-done.7, f32[16,8,128]{2,1,0:T(8,128)} %copy-done.6, ...), custom_call_target="tpu_custom_call" | custom-call | flops 268435456 | bytes 4194304 | tf_op jit(solution)/shard_map/pallas_call | solution.py:412
  (10 shorter events, 0.1 us)
Async XLA Ops:
  2.5 9.2 %collective-permute-start = (f32[512,128]{1,0:T(8,128)S(1)}, f32[512,128]{1,0:T(8,128)S(1)}, u32[]{:S(2)}, u32[]{:S(2)}) collective-permute-start(f32[512,128]{1,0:T(8,128)S(1)} %get-tuple-element.26), channel_id=1, source_target_pairs={{0,1},{32,33},{64,65},{96,97},{128,129},{160,161},{192,193},{224,2... | collective-permute-start | bytes 786440 | tf_op jit(solution)/shard_map/ppermute | solution.py:345
  3.9 143.6 %copy-start.5 = (s32[4]{0:T(128)}, s32[4]{0:T(128)S(1)}, u32[]{:S(2)}) copy-start(s32[4]{0:T(128)S(1)} %pad_add_fusion.place) | copy-start | bytes 52
  13.4 14.6 %all-to-all-start = ((f32[16,48,128]{2,1,0:T(8,128)}), f32[16,48,128]{2,1,0:T(8,128)S(1)}, u32[]{:S(2)}, u32[]{:S(2)}) async-start(f32[16,48,128]{2,1,0:T(8,128)} %shard_map.31), calls=%async_computation | async-start | bytes 786432 | tf_op jit(solution)/shard_map/all_to_all | solution.py:294
  20.3 56.6 %copy-start = (f32[1024,512]{1,0:T(8,128)}, f32[1024,512]{1,0:T(8,128)S(1)}, u32[]{:S(2)}) copy-start(f32[1024,512]{1,0:T(8,128)S(1)} %get-tuple-element.13.matrix_ref) | copy-start | bytes 6291460
  28.8 21.4 %all-to-all-start.1 = ((f32[16,48,128]{2,1,0:T(8,128)}), f32[16,48,128]{2,1,0:T(8,128)S(1)}, u32[]{:S(2)}, u32[]{:S(2)}) async-start(f32[16,48,128]{2,1,0:T(8,128)} %pad_maximum_fusion), calls=%async_computation.1 | async-start | bytes 786432 | tf_op jit(solution)/shard_map/all_to_all | solution.py:288
  66.6 8.1 %collective-permute-start.1 = (f32[16,48,128]{2,1,0:T(8,128)S(1)}, f32[16,48,128]{2,1,0:T(8,128)S(1)}, u32[]{:S(2)}, u32[]{:S(2)}) collective-permute-start(f32[16,48,128]{2,1,0:T(8,128)S(1)} %all_to_all.35.own_ref), channel_id=1, source_target_pairs={{0,1},{1,0},{2,3},{3,2},{4,5},{5,4},{6,7},{7,6},{8,9},{9,8},{10,11... | collective-permute-start | bytes 1179656 | tf_op jit(solution)/shard_map/ppermute | solution.py:299
  76.9 21.5 %all-to-all-start.3 = ((f32[16,64,128]{2,1,0:T(8,128)}), f32[16,64,128]{2,1,0:T(8,128)S(1)}, u32[]{:S(2)}, u32[]{:S(2)}) async-start(f32[16,64,128]{2,1,0:T(8,128)} %get-tuple-element.15), calls=%async_computation.3 | async-start | bytes 1048576 | tf_op jit(solution)/shard_map/all_to_all | solution.py:288
  94.3 55.3 %copy-start.1 = (f32[768,128]{1,0:T(8,128)}, f32[768,128]{1,0:T(8,128)S(1)}, u32[]{:S(2)}) copy-start(f32[768,128]{1,0:T(8,128)S(1)} %shard_map.33.factors_ref.triangle_ref.band_ref) | copy-start | bytes 1179652
  100.2 17.9 %all-to-all-start.4 = ((f32[16,40,128]{2,1,0:T(8,128)}), f32[16,40,128]{2,1,0:T(8,128)S(1)}, u32[]{:S(2)}, u32[]{:S(2)}) async-start(f32[16,40,128]{2,1,0:T(8,128)} %get-tuple-element.17), calls=%async_computation.4 | async-start | bytes 655360 | tf_op jit(solution)/shard_map/all_to_all | solution.py:288
  105.3 18.4 %collective-permute-start.3 = (f32[32,128]{1,0:T(8,128)S(1)}, f32[32,128]{1,0:T(8,128)S(1)}, u32[]{:S(2)}, u32[]{:S(2)}) collective-permute-start(f32[32,128]{1,0:T(8,128)S(1)} %get-tuple-element.19), channel_id=1, source_target_pairs={{256,0},{288,1},{320,2},{352,3},{384,4},{416,5},{448,6},{480,7},{0... | collective-permute-start | bytes 49160 | tf_op jit(solution)/shard_map/ppermute | solution.py:315
  118.1 38.8 %copy-start.2 = (f32[16,40,128]{2,1,0:T(8,128)}, f32[16,40,128]{2,1,0:T(8,128)S(1)}, u32[]{:S(2)}) copy-start(f32[16,40,128]{2,1,0:T(8,128)S(1)} %all-to-all-done.4.found_ref.cols_ref) | copy-start | bytes 983044
  118.2 6.3 %collective-permute-start.2 = (f32[8,128]{1,0:T(8,128)S(1)}, f32[8,128]{1,0:T(8,128)S(1)}, u32[]{:S(2)}, u32[]{:S(2)}) collective-permute-start(f32[8,128]{1,0:T(8,128)S(1)} %slice_reduce_fusion.1), channel_id=1, source_target_pairs={{0,1},{1,0},{2,3},{3,2},{4,5},{5,4},{6,7},{7,6},{8,9},{9,8},{10,11... | collective-permute-start | bytes 12296 | tf_op jit(solution)/shard_map/ppermute | solution.py:299
  139.9 17.0 %copy-start.3 = (f32[16,32,128]{2,1,0:T(8,128)}, f32[16,32,128]{2,1,0:T(8,128)S(1)}, u32[]{:S(2)}) copy-start(f32[16,32,128]{2,1,0:T(8,128)S(1)} %get-tuple-element.22.own_ref) | copy-start | bytes 786436
  139.9 17.0 %collective-permute-start.4 = (f32[16,32,128]{2,1,0:T(8,128)S(1)}, f32[16,32,128]{2,1,0:T(8,128)S(1)}, u32[]{:S(2)}, u32[]{:S(2)}) collective-permute-start(f32[16,32,128]{2,1,0:T(8,128)S(1)} %get-tuple-element.22.own_ref), channel_id=1, source_target_pairs={{0,1},{1,0},{2,3},{3,2},{4,5},{5,4},{6,7},{7,6},{8,9},{9,8},{10,11... | collective-permute-start | bytes 786440 | tf_op jit(solution)/shard_map/ppermute | solution.py:299
  144.0 13.0 %all-to-all-start.6 = ((f32[16,8,128]{2,1,0:T(8,128)}), f32[16,8,128]{2,1,0:T(8,128)S(1)}, u32[]{:S(2)}, u32[]{:S(2)}) async-start(f32[16,8,128]{2,1,0:T(8,128)} %get-tuple-element.20.ready_ref), calls=%async_computation.6 | async-start | bytes 131072 | tf_op jit(solution)/shard_map/all_to_all | solution.py:288
  149.6 0.7 copy-start.4
  156.9 0.6 copy-start.6
  157.0 0.7 copy-start.7

commit v4 on v3

--- a/solution.py
+++ b/solution.py
@@ -4,9 +4,10 @@
 from jax import lax
 from jax.experimental import pallas as pl
 from jax.experimental.pallas import tpu as pltpu
-from jax.sharding import PartitionSpec as P
+from jax.sharding import Mesh, PartitionSpec as P
 
 CLOSING = 2
+COL = ("pair", "core")
 
 
 def product(first, second, first_dim=1, second_dim=0):
@@ -161,22 +162,32 @@
     out_ref[:, mine:, :] = coupling.reshape(count, wide, size)
 
 
-def gather_kernel(found_ref, other_ref, scaled_ref, out_ref):
+def gather_kernel(found_ref, scaled_ref, out_ref):
     mine = scaled_ref.shape[0]
     count = out_ref.shape[0]
     out_ref[:, :mine, :] = jnp.broadcast_to(scaled_ref[...][None], (count,) + scaled_ref.shape)
-    pieces = found_ref[:, mine:, :].sum(axis=0) + other_ref[...]
+    pieces = found_ref[:, mine:, :].sum(axis=0)
     out_ref[:, mine:, :] = jnp.broadcast_to(pieces[None], (count,) + pieces.shape)
 
 
 def coupling_kernel(part_ref, out_ref, scaled_ref):
     mine = scaled_ref.shape[1]
+    scaled_ref[...] = part_ref[:, :mine, :]
     pieces = part_ref[:, mine:, :].sum(axis=0)
     out_ref[...] = jnp.broadcast_to(pieces[None], out_ref.shape)
-    scaled_ref[...] = part_ref[:, :mine, :]
-
-
-def reflect_kernel(place, panel_ref, chunks_ref, factors_ref, ready_ref, rows_ref, cols_ref):
+
+
+def reflect_kernel(
+    place,
+    panel_ref,
+    chunks_ref,
+    factors_ref,
+    ready_ref,
+    rows_ref,
+    cols_ref,
+    high_ref,
+    low_ref,
+):
     del ready_ref
     size = factors_ref.shape[1]
     mine = chunks_ref.shape[1] // 2
@@ -192,6 +203,11 @@
     @pl.when(place[1] == 1)
     def _():
         cols_ref[:size] = unit_lower
+
+    triangle = halves(factors_ref[4 * size : 5 * size])
+    high, low = halves(passes(halves(cols_ref[...]), triangle, 1, 1))
+    high_ref[...] = high
+    low_ref[...] = low
 
 
 def close_kernel(
@@ -203,7 +219,8 @@
     other_ref,
     coupling_ref,
     reflect_ref,
-    triangle_ref,
+    turned_high_ref,
+    turned_low_ref,
     band_ref,
     out_ref,
     high,
@@ -220,12 +237,11 @@
 
     @pl.when(step == 0)
     def _():
-        coupling = coupling_ref[...].reshape(size, size)
-        correction = product(triangle_ref[...], coupling, 0, 0)
-        reflect_cols = reflect_cols_ref[...]
+        cores = coupling_ref[...].reshape(-1, 2, coupling_ref.shape[1], size)
+        coupling = halves((cores[:, 0] + cores[:, 1]).reshape(size, size))
         scaled_cols = cols_ref[:, :mine, :].reshape(-1, size)
-        update = scaled_cols - passes(halves(reflect_cols), halves(correction))
-        right = halves(jnp.concatenate([update, reflect_cols], axis=1))
+        update = scaled_cols - passes((turned_high_ref[...], turned_low_ref[...]), coupling)
+        right = halves(jnp.concatenate([update, reflect_cols_ref[...]], axis=1))
         high[...] = right[0]
         low[...] = right[1]
 
@@ -284,19 +300,12 @@
     )(base)
 
 
-def exchange(array):
-    return lax.all_to_all(array, "row", 0, 0)
-
-
-def same_core(array):
-    count = lax.axis_size("col")
-    groups = [list(range(core, count, 2)) for core in range(2)]
-    return lax.all_to_all(array, "col", 0, 0, axis_index_groups=groups)
+def exchange(array, axis):
+    return lax.all_to_all(array, axis, 0, 0)
 
 
 def flip(array):
-    count = lax.axis_size("col")
-    return lax.ppermute(array, "col", [(i, i ^ 1) for i in range(count)])
+    return lax.ppermute(array, "core", [(0, 1), (1, 0)])
 
 
 def to_all(array, count):
@@ -305,21 +314,21 @@
 
 def to_rows(chunk):
     rows_count = lax.axis_size("row")
-    cols_count = lax.axis_size("col")
+    cols_count = lax.axis_size(COL)
     pairs = []
     for row in range(rows_count):
         for col in range(cols_count):
             half, k = divmod(col, rows_count)
             source = (k + rows_count // 2) % rows_count * cols_count + half * rows_count + row
             pairs.append((source, row * cols_count + col))
-    return lax.ppermute(chunk, ("row", "col"), pairs)
+    return lax.ppermute(chunk, ("row",) + COL, pairs)
 
 
 def on_device(matrix):
     rows_count = lax.axis_size("row")
-    cols_count = lax.axis_size("col")
+    cols_count = lax.axis_size(COL)
     row_place = lax.axis_index("row")
-    col_place = lax.axis_index("col")
+    col_place = lax.axis_index(COL)
     local_blocks = matrix.shape[0]
     size = matrix.shape[2]
     column_blocks = matrix.shape[3]
@@ -342,8 +351,8 @@
         in_specs=[SCALARS, WHOLE, WHOLE],
         compiler_params=ROOM,
         cost_estimate=cost(rows * size * size, 8 * rows * size),
-    )(place, panel[: rows // 2], lax.ppermute(panel[rows // 2 :], "col", [(0, 1)]))
-    found = same_core(opening)[0]
+    )(place, panel[: rows // 2], lax.ppermute(panel[rows // 2 :], COL, [(0, 1)]))
+    found = exchange(opening, "pair")[0]
     local_part, strip = pl.pallas_call(
         strip_kernel,
         grid=(column_blocks,),
@@ -359,11 +368,13 @@
         compiler_params=ROOM,
         cost_estimate=cost(0, 8 * rows * cols),
     )(place, table)
-    summed = exchange(jnp.concatenate([strip, to_all(found[mine:], rows_count)], axis=1))
+    summed = exchange(
+        jnp.concatenate([strip, to_all(found[mine:], rows_count)], axis=1), "row"
+    )
     panel_chunk = summed[0, :mine]
     second_chunk = summed[1, :mine]
     square = summed[:, mine:].sum(axis=0)
-    own = same_core(to_all(jnp.concatenate([found[:mine], square], axis=0), pairs))
+    own = exchange(to_all(jnp.concatenate([found[:mine], square], axis=0), pairs), "pair")
     other = flip(own)
 
     images, panel_rows, base = pl.pallas_call(
@@ -373,7 +384,7 @@
         compiler_params=ROOM,
         cost_estimate=cost(2 * rows * cols * size, 4 * rows * (cols + 3 * size)),
     )(place, own, other, local_part, panel_chunk)
-    chunks = exchange(images)
+    chunks = exchange(images, "row")
     packed = factors(base)
 
     middle, scaled = pl.pallas_call(
@@ -384,29 +395,30 @@
         cost_estimate=cost(2 * mine * size * size * 5, 8 * rows * size),
     )(place, chunks, panel_chunk, second_chunk, packed)
     scaled = to_rows(scaled)
-    at_cols = exchange(middle)
+    at_cols = exchange(middle, "row")
 
     gathering = pl.pallas_call(
         gather_kernel,
         out_shape=struct(pairs, mine + wide, size),
         compiler_params=ROOM,
         cost_estimate=cost(0, 4 * rows * size),
-    )(at_cols, flip(at_cols[:, mine:].sum(axis=0)), scaled)
-    part = same_core(gathering)
-    coupling, part = pl.pallas_call(
+    )(at_cols, scaled)
+    part = exchange(gathering, "pair")
+    sums, part = pl.pallas_call(
         coupling_kernel,
-        out_shape=(struct(rows_count, wide, size), struct(pairs, mine, size)),
+        out_shape=(struct(2 * rows_count, wide, size), struct(pairs, mine, size)),
         compiler_params=ROOM,
         cost_estimate=cost(0, 4 * rows * size),
     )(part)
-    reflect_rows, reflect_cols = pl.pallas_call(
+    coupling = exchange(sums, ("row", "core"))
+    halved = jax.ShapeDtypeStruct((cols, size), jnp.bfloat16)
+    reflect_rows, reflect_cols, high, low = pl.pallas_call(
         reflect_kernel,
-        out_shape=(struct(rows, size), struct(cols, size)),
+        out_shape=(struct(rows, size), struct(cols, size), halved, halved),
         in_specs=[SCALARS, WHOLE, WHOLE, WHOLE, pl.BlockSpec(memory_space=pl.ANY)],
         compiler_params=ROOM,
         cost_estimate=cost(4 * rows * size * size, 8 * rows * size),
-    )(place, panel_rows, chunks, packed, coupling)
-    coupling = exchange(coupling)
+    )(place, panel_rows, chunks, packed, sums)
     rest = flip(part)
     extent = ratio * size * max(1, column_blocks // CLOSING)
     banded = pl.pallas_call(
@@ -420,9 +432,10 @@
             entire(reflect_cols),
             entire(part),
             entire(rest),
-            entire(coupling),
+            WHOLE,
             pl.BlockSpec((extent, size), lambda i: (i, 0)),
-            pl.BlockSpec((size, size), lambda i: (4, 0)),
+            entire(high),
+            entire(low),
             pl.BlockSpec((size, size), lambda i: (5, 0)),
         ],
         out_specs=pl.BlockSpec((extent, column_blocks, size), lambda i: (i, 0, 0)),
@@ -432,7 +445,19 @@
         ],
         compiler_params=MORE,
         cost_estimate=cost(4 * rows * cols * size, 8 * rows * cols),
-    )(place, local_part, at_cols, reflect_cols, part, rest, coupling, reflect_rows, packed, packed)
+    )(
+        place,
+        local_part,
+        at_cols,
+        reflect_cols,
+        part,
+        rest,
+        coupling,
+        reflect_rows,
+        high,
+        low,
+        packed,
+    )
     return (
         banded.reshape(matrix.shape),
         reflect_rows.reshape(local_blocks, 1, size, size),
@@ -440,8 +465,14 @@
 
 
 def solution(mesh):
-    in_specs = (P(None, "row", None, None, "col", None),)
-    out_specs = (P(None, "row", None, None, "col", None), P(None, "row", None, None))
+    rows_count, cols_count = mesh.devices.shape
+    devices = mesh.devices.reshape(rows_count, cols_count // 2, 2)
+    in_specs = (P(None, "row", None, None, COL, None),)
+    out_specs = (P(None, "row", None, None, COL, None), P(None, "row", None, None))
     return jax.shard_map(
-        on_device, mesh=mesh, in_specs=in_specs, out_specs=out_specs, check_vma=False
-    )
+        on_device,
+        mesh=Mesh(devices, ("row",) + COL),
+        in_specs=in_specs,
+        out_specs=out_specs,
+        check_vma=False,
+    )

time: 164 us -> 162 us (0.988)
  blocking collectives: 31.1 us -> 27.2 us
  waiting for transfers between devices: 45.3 us -> 47.7 us
    ppermute x5 -> x4, waiting for transfers between devices: 9.91 us -> 17.2 us  [the longest x1 8.06 us: to_rows(): return lax.ppermute(chunk, ('row',) + COL, pairs)]
    all_to_all x5, waiting for transfers between devices: 35.4 us -> 30.5 us  [exchange(): return lax.all_to_all(array, axis, 0, 0)]
    all_to_all x2, blocking collectives: 31.1 us -> 27.2 us  [exchange(): return lax.all_to_all(array, axis, 0, 0)]
    ppermute x5 -> x4, starting transfers between devices: 25.8 us -> 22.2 us  [the longest x2 12.8 us: flip(): return lax.ppermute(array, 'core', [(0, 1), (1, 0)])]
    all_to_all x5, starting transfers between devices: 25.1 us -> 27.5 us  [exchange(): return lax.all_to_all(array, axis, 0, 0)]
    unnamed x17 -> x21, local copies, waits for them, and re-layouts: 3.26 us -> 4.61 us
  transfers between devices with their start and end apart: 10 -> 9, of which waited for: 8 -> 7; matrix products, arithmetic and copies ran while one was open for 1% -> 1% of each run, Pallas kernels for 11% -> 11%
where the time goes in v4:
time: 162 us
  starting transfers between devices  49.7 us (31%)
  waiting for transfers between devices  47.7 us (29%)
  Pallas kernels  29.4 us (18%)
  blocking collectives  27.2 us (17%)
  local copies, waits for them, and re-layouts  6.05 us (4%)
    all_to_all x5, waiting for transfers between devices, exchange(): return lax.all_to_all(array, axis, 0, 0)  30.5 us
    all_to_all x5, starting transfers between devices, exchange(): return lax.all_to_all(array, axis, 0, 0)  27.5 us
    all_to_all x2, blocking collectives, exchange(): return lax.all_to_all(array, axis, 0, 0)  27.2 us
    pallas_call x1, Pallas kernels, factors(): pl.pallas_call(factor_kernel, out_shape=struct(6 * size, size), compiler_...  13.5 us
    ppermute x2, starting transfers between devices, flip(): return lax.ppermute(array, 'core', [(0, 1), (1, 0)])  12.8 us
    ppermute x1, starting transfers between devices, to_rows(): return lax.ppermute(chunk, ('row',) + COL, pairs)  8.13 us
    ppermute x1, waiting for transfers between devices, to_rows(): return lax.ppermute(chunk, ('row',) + COL, pairs)  8.06 us
    ppermute x1, waiting for transfers between devices, on_device(): lax.ppermute(panel[rows // 2:], COL, [(0, 1)])  7.8 us
  transfers between devices with their start and end apart: 9, of which 7 were waited for; matrix products, arithmetic and copies ran while one was open for 1% of the time, Pallas kernels for 11%

profile of v4, /device:TPU:1, one launch (start us, length us, event | category | flops | bytes accessed | tf_op | source)
XLA Modules:
  0.0 161.7 jit_solution(16022198047214143381)
XLA Ops:
  0.6 1.8 %copy.3 = f32[8,1,128,4,1,128]{5,2,0,3,4,1:T(8,128)S(1)} copy(f32[8,1,128,4,1,128]{5,4,3,2,1,0:T(1,128)} %param.1) | data formatting | bytes 4194304 | tf_op args[0]
  2.5 1.3 collective-permute-start
  3.8 0.1 pad_add_fusion.place
  3.9 0.0 copy-start.7
  3.9 7.8 %collective-permute-done.other_ref = f32[512,128]{1,0:T(8,128)S(1)} collective-permute-done((f32[512,128]{1,0:T(8,128)S(1)}, f32[512,128]{1,0:T(8,128)S(1)}, u32[]{:S(2)}, u32[]{:S(2)}) %collective-permute-start) | collective-permute-done | bytes 262176 | tf_op jit(solution)/shard_map/ppermute | solution.py:354
  11.7 1.7 %shard_map.31 = f32[16,48,128]{2,1,0:T(8,128)} custom-call(s32[4]{0:T(128)S(1)} %pad_add_fusion.place, f32[512,128]{1,0:T(8,128)S(1)} %get-tuple-element.31.own_ref, f32[512,128]{1,0:T(8,128)S(1)} %collective-permute-done.other_ref), custom_call_target="tpu_custom_call" | custom-call | flops 16777216 | bytes 1048576 | tf_op jit(solution)/shard_map/pallas_call | solution.py:348
  13.4 3.6 %all-to-all-start = ((f32[16,48,128]{2,1,0:T(8,128)}), f32[16,48,128]{2,1,0:T(8,128)S(1)}, u32[]{:S(2)}, u32[]{:S(2)}) async-start(f32[16,48,128]{2,1,0:T(8,128)} %shard_map.31), calls=%async_computation | async-start | bytes 786432 | tf_op jit(solution)/shard_map/all_to_all | solution.py:304
  17.0 1.4 copy.4.matrix_ref
  18.3 1.9 %shard_map.30 = (f32[1024,512]{1,0:T(8,128)S(1)}, f32[16,32,128]{2,1,0:T(8,128)S(1)}) custom-call(s32[4]{0:T(128)S(1)} %pad_add_fusion.place, f32[1024,4,128]{2,1,0:T(4,128)S(1)} %copy.4.matrix_ref), custom_call_target="tpu_custom_call" | custom-call | bytes 4194304 | tf_op jit(solution)/shard_map/pallas_call | solution.py:356
  20.3 0.0 copy-start
  20.3 7.7 %all-to-all-done = f32[16,48,128]{2,1,0:T(8,128)S(1)} async-done(((f32[16,48,128]{2,1,0:T(8,128)}), f32[16,48,128]{2,1,0:T(8,128)S(1)}, u32[]{:S(2)}, u32[]{:S(2)}) %all-to-all-start) | async-done | bytes 393248 | tf_op jit(solution)/shard_map/all_to_all | solution.py:304
  28.0 0.8 pad_maximum_fusion
  28.8 9.0 %all-to-all-start.1 = ((f32[16,48,128]{2,1,0:T(8,128)}), f32[16,48,128]{2,1,0:T(8,128)S(1)}, u32[]{:S(2)}, u32[]{:S(2)}) async-start(f32[16,48,128]{2,1,0:T(8,128)} %pad_maximum_fusion), calls=%async_computation.1 | async-start | bytes 786432 | tf_op jit(solution)/shard_map/all_to_all | solution.py:304
  37.8 12.3 %all-to-all-done.1 = f32[16,48,128]{2,1,0:T(8,128)S(1)} async-done(((f32[16,48,128]{2,1,0:T(8,128)}), f32[16,48,128]{2,1,0:T(8,128)S(1)}, u32[]{:S(2)}, u32[]{:S(2)}) %all-to-all-start.1) | async-done | bytes 393248 | tf_op jit(solution)/shard_map/all_to_all | solution.py:304
  50.2 16.4 %all_to_all.35.own_ref = f32[16,48,128]{2,1,0:T(8,128)S(1)} all-to-all(f32[16,48,128]{2,1,0:T(8,128)S(1)} %broadcast_in_dim.16), channel_id=1, replica_groups=mesh['row'=16,'pair'=16,'core'=2] {'pair'}, dimensions={0} | all-to-all | bytes 786432 | tf_op jit(solution)/shard_map/all_to_all | solution.py:304
  66.6 6.8 %collective-permute-start.1 = (f32[16,48,128]{2,1,0:T(8,128)S(1)}, f32[16,48,128]{2,1,0:T(8,128)S(1)}, u32[]{:S(2)}, u32[]{:S(2)}) collective-permute-start(f32[16,48,128]{2,1,0:T(8,128)S(1)} %all_to_all.35.own_ref), channel_id=1, source_target_pairs={{0,1},{1,0},{2,3},{3,2},{4,5},{5,4},{6,7},{7,6},{8,9},{9,8},{10,11... | collective-permute-start | bytes 1179656 | tf_op jit(solution)/shard_map/ppermute | solution.py:308
  73.4 1.3 collective-permute-done.1.other_ref
  74.8 2.2 %shard_map.32 = (f32[16,64,128]{2,1,0:T(8,128)}, f32[1024,128]{1,0:T(8,128)S(1)}, f32[256,128]{1,0:T(8,128)S(1)}) custom-call(s32[4]{0:T(128)S(1)} %pad_add_fusion.place, f32[16,48,128]{2,1,0:T(8,128)S(1)} %all_to_all.35.own_ref, f32[16,48,128]{2,1,0:T(8,128)S(1)} %collective-permute-done.1.other_ref, f32[1024,512]{1,0:T(8,128)S(1)} %get-tuple-element.15.matrix_ref, ...), custom_call_target="tpu_custom_call" | custom-call | flops 134217728 | bytes 3670016 | tf_op jit(solution)/shard_map/pallas_call | solution.py:380
  76.9 0.0 copy-done
  76.9 3.9 %all-to-all-start.3 = ((f32[16,64,128]{2,1,0:T(8,128)}), f32[16,64,128]{2,1,0:T(8,128)S(1)}, u32[]{:S(2)}, u32[]{:S(2)}) async-start(f32[16,64,128]{2,1,0:T(8,128)} %get-tuple-element.17), calls=%async_computation.3 | async-start | bytes 1048576 | tf_op jit(solution)/shard_map/all_to_all | solution.py:304
  80.9 13.5 %shard_map.33.factors_ref.band_ref = f32[768,128]{1,0:T(8,128)S(1)} custom-call(f32[256,128]{1,0:T(8,128)S(1)} %get-tuple-element.18.base_ref), custom_call_target="tpu_custom_call" | custom-call | flops 268435456 | bytes 33554432 | tf_op jit(solution)/shard_map/pallas_call | solution.py:295
  94.3 0.0 copy-start.1
  94.3 4.0 %all-to-all-done.3.found_ref.chunks_ref = f32[16,64,128]{2,1,0:T(8,128)S(1)} async-done(((f32[16,64,128]{2,1,0:T(8,128)}), f32[16,64,128]{2,1,0:T(8,128)S(1)}, u32[]{:S(2)}, u32[]{:S(2)}) %all-to-all-start.3) | async-done | bytes 524320 | tf_op jit(solution)/shard_map/all_to_all | solution.py:304
  98.4 1.9 %shard_map.34 = (f32[16,40,128]{2,1,0:T(8,128)}, f32[32,128]{1,0:T(8,128)S(1)}) custom-call(s32[4]{0:T(128)S(1)} %pad_add_fusion.place, f32[16,64,128]{2,1,0:T(8,128)S(1)} %all-to-all-done.3.found_ref.chunks_ref, f32[32,128]{1,0:T(8,128)S(1)} %get-tuple-element.33.chunk_ref.panel_ref, f32[32,128]{1,0:T(8,128)S(1)} %get-tuple-element.32.second_ref, ...), custom_call_target="tpu_custom_call" | custom-call | flops 5242880 | bytes 1048576 | tf_op jit(solution)/shard_map/pallas_call | solution.py:390
  100.2 5.0 %all-to-all-start.4 = ((f32[16,40,128]{2,1,0:T(8,128)}), f32[16,40,128]{2,1,0:T(8,128)S(1)}, u32[]{:S(2)}, u32[]{:S(2)}) async-start(f32[16,40,128]{2,1,0:T(8,128)} %get-tuple-element.19), calls=%async_computation.4 | async-start | bytes 655360 | tf_op jit(solution)/shard_map/all_to_all | solution.py:304
  105.3 8.1 %collective-permute-start.2 = (f32[32,128]{1,0:T(8,128)S(1)}, f32[32,128]{1,0:T(8,128)S(1)}, u32[]{:S(2)}, u32[]{:S(2)}) collective-permute-start(f32[32,128]{1,0:T(8,128)S(1)} %get-tuple-element.21), channel_id=1, source_target_pairs={{256,0},{288,1},{320,2},{352,3},{384,4},{416,5},{448,6},{480,7},{0... | collective-permute-start | bytes 49160 | tf_op jit(solution)/shard_map/ppermute | solution.py:324
  113.4 8.1 %collective-permute-done.2.scaled_ref = f32[32,128]{1,0:T(8,128)S(1)} collective-permute-done((f32[32,128]{1,0:T(8,128)S(1)}, f32[32,128]{1,0:T(8,128)S(1)}, u32[]{:S(2)}, u32[]{:S(2)}) %collective-permute-start.2) | collective-permute-done | bytes 16416 | tf_op jit(solution)/shard_map/ppermute | solution.py:324
  121.5 0.0 all-to-all-done.4.found_ref.cols_ref
  121.5 0.0 copy-start.2
  121.5 10.8 %all_to_all.36.part_ref = f32[16,40,128]{2,1,0:T(8,128)S(1)} all-to-all(f32[16,40,128]{2,1,0:T(8,128)S(1)} %shard_map.35), channel_id=1, replica_groups=mesh['row'=16,'pair'=16,'core'=2] {'pair'}, dimensions={0} | all-to-all | bytes 655360 | tf_op jit(solution)/shard_map/all_to_all | solution.py:304
  132.3 0.7 shard_map.36
  133.0 0.0 copy-start.3
  133.0 5.9 %collective-permute-start.3 = (f32[16,32,128]{2,1,0:T(8,128)S(1)}, f32[16,32,128]{2,1,0:T(8,128)S(1)}, u32[]{:S(2)}, u32[]{:S(2)}) collective-permute-start(f32[16,32,128]{2,1,0:T(8,128)S(1)} %get-tuple-element.24.own_ref), channel_id=1, source_target_pairs={{0,1},{1,0},{2,3},{3,2},{4,5},{5,4},{6,7},{7,6},{8,9},{9,8},{10,11... | collective-permute-start | bytes 786440 | tf_op jit(solution)/shard_map/ppermute | solution.py:308
  138.9 5.9 %all-to-all-start.6 = ((f32[32,8,128]{2,1,0:T(8,128)}), f32[32,8,128]{2,1,0:T(8,128)S(1)}, u32[]{:S(2)}, u32[]{:S(2)}) async-start(f32[32,8,128]{2,1,0:T(8,128)} %get-tuple-element.22.ready_ref), calls=%async_computation.6 | async-start | bytes 262144 | tf_op jit(solution)/shard_map/all_to_all | solution.py:304
  144.9 0.0 copy-done.7
  144.9 2.3 %shard_map.37 = (f32[1024,128]{1,0:T(8,128)}, f32[512,128]{1,0:T(8,128)S(1)}, bf16[512,128]{1,0:T(8,128)(2,1)S(1)}, bf16[512,128]{1,0:T(8,128)(2,1)S(1)}) custom-call(s32[4]{0:T(128)S(1)} %pad_add_fusion.place, f32[1024,128]{1,0:T(8,128)S(1)} %get-tuple-element.20.panel_ref, f32[16,64,128]{2,1,0:T(8,128)S(1)} %all-to-all-done.3.found_ref.chunks_ref, ...), custom_call_target="tpu_custom_call" | custom-call | flops 67108864 | bytes 1048576 | tf_op jit(solution)/shard_map/pallas_call | solution.py:415
  147.2 0.0 copy-done.1
  147.2 0.0 copy-start.4
  147.2 0.7 copy-done.4
  147.9 0.0 copy-start.5
  147.9 0.7 copy-done.5
  148.6 0.0 copy-start.6
  148.6 0.6 copy-done.6
  149.2 6.4 %all-to-all-done.6.coupling_ref = f32[32,8,128]{2,1,0:T(8,128)S(1)} async-done(((f32[32,8,128]{2,1,0:T(8,128)}), f32[32,8,128]{2,1,0:T(8,128)S(1)}, u32[]{:S(2)}, u32[]{:S(2)}) %all-to-all-start.6) | async-done | bytes 131104 | tf_op jit(solution)/shard_map/all_to_all | solution.py:304
  155.6 0.0 copy-start.8
  155.6 0.0 collective-permute-done.3.other_ref
  155.7 0.0 copy-start.9
  155.7 0.0 copy-done.2
  155.7 0.0 copy-done.3
  155.7 0.6 copy-done.8
  156.3 0.1 copy-done.9
  156.4 5.3 %shard_map.38 = f32[1024,4,128]{2,1,0:T(4,128)} custom-call(s32[4]{0:T(128)} %copy-done.7, f32[1024,512]{1,0:T(8,128)} %copy-done, f32[16,40,128]{2,1,0:T(8,128)} %copy-done.2, f32[512,128]{1,0:T(8,128)} %copy-done.4, f32[16,32,128]{2,1,0:T(8,128)} %copy-done.3, f32[16,32,128]{2,1,0:T(8,128)} %copy-done.9, f32[32,8,128]{2,1,0:T(8,128)} %copy-done.8, ...), custom_call_target="tpu_custom_call" | custom-call | flops 268435456 | bytes 4194304 | tf_op jit(solution)/shard_map/pallas_call | solution.py:424
  (9 shorter events, 0.1 us)
Async XLA Ops:
  2.5 9.2 %collective-permute-start = (f32[512,128]{1,0:T(8,128)S(1)}, f32[512,128]{1,0:T(8,128)S(1)}, u32[]{:S(2)}, u32[]{:S(2)}) collective-permute-start(f32[512,128]{1,0:T(8,128)S(1)} %get-tuple-element.30), channel_id=1, source_target_pairs={{0,1},{32,33},{64,65},{96,97},{128,129},{160,161},{192,193},{224,2... | collective-permute-start | bytes 786440 | tf_op jit(solution)/shard_map/ppermute | solution.py:354
  3.9 141.0 %copy-start.7 = (s32[4]{0:T(128)}, s32[4]{0:T(128)S(1)}, u32[]{:S(2)}) copy-start(s32[4]{0:T(128)S(1)} %pad_add_fusion.place) | copy-start | bytes 52
  13.4 14.6 %all-to-all-start = ((f32[16,48,128]{2,1,0:T(8,128)}), f32[16,48,128]{2,1,0:T(8,128)S(1)}, u32[]{:S(2)}, u32[]{:S(2)}) async-start(f32[16,48,128]{2,1,0:T(8,128)} %shard_map.31), calls=%async_computation | async-start | bytes 786432 | tf_op jit(solution)/shard_map/all_to_all | solution.py:304
  20.3 56.6 %copy-start = (f32[1024,512]{1,0:T(8,128)}, f32[1024,512]{1,0:T(8,128)S(1)}, u32[]{:S(2)}) copy-start(f32[1024,512]{1,0:T(8,128)S(1)} %get-tuple-element.15.matrix_ref) | copy-start | bytes 6291460
  28.8 21.4 %all-to-all-start.1 = ((f32[16,48,128]{2,1,0:T(8,128)}), f32[16,48,128]{2,1,0:T(8,128)S(1)}, u32[]{:S(2)}, u32[]{:S(2)}) async-start(f32[16,48,128]{2,1,0:T(8,128)} %pad_maximum_fusion), calls=%async_computation.1 | async-start | bytes 786432 | tf_op jit(solution)/shard_map/all_to_all | solution.py:304
  66.6 8.1 %collective-permute-start.1 = (f32[16,48,128]{2,1,0:T(8,128)S(1)}, f32[16,48,128]{2,1,0:T(8,128)S(1)}, u32[]{:S(2)}, u32[]{:S(2)}) collective-permute-start(f32[16,48,128]{2,1,0:T(8,128)S(1)} %all_to_all.35.own_ref), channel_id=1, source_target_pairs={{0,1},{1,0},{2,3},{3,2},{4,5},{5,4},{6,7},{7,6},{8,9},{9,8},{10,11... | collective-permute-start | bytes 1179656 | tf_op jit(solution)/shard_map/ppermute | solution.py:308
  76.9 21.4 %all-to-all-start.3 = ((f32[16,64,128]{2,1,0:T(8,128)}), f32[16,64,128]{2,1,0:T(8,128)S(1)}, u32[]{:S(2)}, u32[]{:S(2)}) async-start(f32[16,64,128]{2,1,0:T(8,128)} %get-tuple-element.17), calls=%async_computation.3 | async-start | bytes 1048576 | tf_op jit(solution)/shard_map/all_to_all | solution.py:304
  94.3 52.9 %copy-start.1 = (f32[768,128]{1,0:T(8,128)}, f32[768,128]{1,0:T(8,128)S(1)}, u32[]{:S(2)}) copy-start(f32[768,128]{1,0:T(8,128)S(1)} %shard_map.33.factors_ref.band_ref) | copy-start | bytes 1179652
  100.2 21.3 %all-to-all-start.4 = ((f32[16,40,128]{2,1,0:T(8,128)}), f32[16,40,128]{2,1,0:T(8,128)S(1)}, u32[]{:S(2)}, u32[]{:S(2)}) async-start(f32[16,40,128]{2,1,0:T(8,128)} %get-tuple-element.19), calls=%async_computation.4 | async-start | bytes 655360 | tf_op jit(solution)/shard_map/all_to_all | solution.py:304
  105.3 16.2 %collective-permute-start.2 = (f32[32,128]{1,0:T(8,128)S(1)}, f32[32,128]{1,0:T(8,128)S(1)}, u32[]{:S(2)}, u32[]{:S(2)}) collective-permute-start(f32[32,128]{1,0:T(8,128)S(1)} %get-tuple-element.21), channel_id=1, source_target_pairs={{256,0},{288,1},{320,2},{352,3},{384,4},{416,5},{448,6},{480,7},{0... | collective-permute-start | bytes 49160 | tf_op jit(solution)/shard_map/ppermute | solution.py:324
  121.5 34.2 %copy-start.2 = (f32[16,40,128]{2,1,0:T(8,128)}, f32[16,40,128]{2,1,0:T(8,128)S(1)}, u32[]{:S(2)}) copy-start(f32[16,40,128]{2,1,0:T(8,128)S(1)} %all-to-all-done.4.found_ref.cols_ref) | copy-start | bytes 983044
  133.0 22.7 %copy-start.3 = (f32[16,32,128]{2,1,0:T(8,128)}, f32[16,32,128]{2,1,0:T(8,128)S(1)}, u32[]{:S(2)}) copy-start(f32[16,32,128]{2,1,0:T(8,128)S(1)} %get-tuple-element.24.own_ref) | copy-start | bytes 786436
  133.0 22.7 %collective-permute-start.3 = (f32[16,32,128]{2,1,0:T(8,128)S(1)}, f32[16,32,128]{2,1,0:T(8,128)S(1)}, u32[]{:S(2)}, u32[]{:S(2)}) collective-permute-start(f32[16,32,128]{2,1,0:T(8,128)S(1)} %get-tuple-element.24.own_ref), channel_id=1, source_target_pairs={{0,1},{1,0},{2,3},{3,2},{4,5},{5,4},{6,7},{7,6},{8,9},{9,8},{10,11... | collective-permute-start | bytes 786440 | tf_op jit(solution)/shard_map/ppermute | solution.py:308
  138.9 16.7 %all-to-all-start.6 = ((f32[32,8,128]{2,1,0:T(8,128)}), f32[32,8,128]{2,1,0:T(8,128)S(1)}, u32[]{:S(2)}, u32[]{:S(2)}) async-start(f32[32,8,128]{2,1,0:T(8,128)} %get-tuple-element.22.ready_ref), calls=%async_computation.6 | async-start | bytes 262144 | tf_op jit(solution)/shard_map/all_to_all | solution.py:304
  147.2 0.7 copy-start.4
  147.9 0.7 copy-start.5
  148.6 0.6 copy-start.6
  155.6 0.7 copy-start.8
  155.7 0.8 copy-start.9

commit v5 on v4

--- a/solution.py
+++ b/solution.py
@@ -287,7 +287,7 @@
 
 
 ROOM = pltpu.CompilerParams(vmem_limit_bytes=24 << 20)
-MORE = pltpu.CompilerParams(vmem_limit_bytes=56 << 20)
+MORE = pltpu.CompilerParams(vmem_limit_bytes=50 << 20)
 
 
 def factors(base):

time: 162 us -> 162 us (level)
  waiting for transfers between devices: 47.7 us -> 49.7 us
  local copies, waits for them, and re-layouts: 6.05 us -> 4.33 us
    all_to_all x5, waiting for transfers between devices: 30.5 us -> 32.5 us  [exchange(): return lax.all_to_all(array, axis, 0, 0)]
    unnamed x21 -> x5, local copies, waits for them, and re-layouts: 4.61 us -> 2.89 us
where the time goes in v5:
time: 162 us; the launch traced here: 161 us
  starting transfers between devices  49.7 us (31%)
  waiting for transfers between devices  49.7 us (31%)
  Pallas kernels  28.9 us (18%)
  blocking collectives  27.2 us (17%)
  local copies, waits for them, and re-layouts  4.33 us (3%)
    all_to_all x5, waiting for transfers between devices, exchange(): return lax.all_to_all(array, axis, 0, 0)  32.5 us
    all_to_all x5, starting transfers between devices, exchange(): return lax.all_to_all(array, axis, 0, 0)  27.5 us
    all_to_all x2, blocking collectives, exchange(): return lax.all_to_all(array, axis, 0, 0)  27.2 us
    pallas_call x1, Pallas kernels, factors(): pl.pallas_call(factor_kernel, out_shape=struct(6 * size, size), compiler_...  13.5 us
    ppermute x2, starting transfers between devices, flip(): return lax.ppermute(array, 'core', [(0, 1), (1, 0)])  12.8 us
    ppermute x1, starting transfers between devices, to_rows(): return lax.ppermute(chunk, ('row',) + COL, pairs)  8.13 us
    ppermute x1, waiting for transfers between devices, to_rows(): return lax.ppermute(chunk, ('row',) + COL, pairs)  8.06 us
    ppermute x1, waiting for transfers between devices, on_device(): lax.ppermute(panel[rows // 2:], COL, [(0, 1)])  7.8 us
  transfers between devices with their start and end apart: 9, of which 7 were waited for; matrix products, arithmetic and copies ran while one was open for 1% of the time, Pallas kernels for 11%

profile of v5, /device:TPU:1, one launch (start us, length us, event | category | flops | bytes accessed | tf_op | source)
XLA Modules:
  0.0 161.4 jit_solution(12922307265223624176)
XLA Ops:
  0.6 1.8 %copy.3 = f32[8,1,128,4,1,128]{5,2,0,3,4,1:T(8,128)S(1)} copy(f32[8,1,128,4,1,128]{5,4,3,2,1,0:T(1,128)} %param.1) | data formatting | bytes 4194304 | tf_op args[0]
  2.5 1.3 collective-permute-start
  3.8 0.1 pad_add_fusion.place
  3.9 7.8 %collective-permute-done.other_ref = f32[512,128]{1,0:T(8,128)S(1)} collective-permute-done((f32[512,128]{1,0:T(8,128)S(1)}, f32[512,128]{1,0:T(8,128)S(1)}, u32[]{:S(2)}, u32[]{:S(2)}) %collective-permute-start) | collective-permute-done | bytes 262176 | tf_op jit(solution)/shard_map/ppermute | solution.py:354
  11.7 1.7 %shard_map.31 = f32[16,48,128]{2,1,0:T(8,128)} custom-call(s32[4]{0:T(128)S(1)} %pad_add_fusion.place, f32[512,128]{1,0:T(8,128)S(1)} %get-tuple-element.31.own_ref, f32[512,128]{1,0:T(8,128)S(1)} %collective-permute-done.other_ref), custom_call_target="tpu_custom_call" | custom-call | flops 16777216 | bytes 1048576 | tf_op jit(solution)/shard_map/pallas_call | solution.py:348
  13.4 3.6 %all-to-all-start = ((f32[16,48,128]{2,1,0:T(8,128)}), f32[16,48,128]{2,1,0:T(8,128)S(1)}, u32[]{:S(2)}, u32[]{:S(2)}) async-start(f32[16,48,128]{2,1,0:T(8,128)} %shard_map.31), calls=%async_computation | async-start | bytes 786432 | tf_op jit(solution)/shard_map/all_to_all | solution.py:304
  17.0 1.4 copy.4.matrix_ref
  18.3 1.9 %shard_map.30 = (f32[1024,512]{1,0:T(8,128)S(1)}, f32[16,32,128]{2,1,0:T(8,128)S(1)}) custom-call(s32[4]{0:T(128)S(1)} %pad_add_fusion.place, f32[1024,4,128]{2,1,0:T(4,128)S(1)} %copy.4.matrix_ref), custom_call_target="tpu_custom_call" | custom-call | bytes 4194304 | tf_op jit(solution)/shard_map/pallas_call | solution.py:356
  20.3 0.0 copy-start
  20.3 7.7 %all-to-all-done = f32[16,48,128]{2,1,0:T(8,128)S(1)} async-done(((f32[16,48,128]{2,1,0:T(8,128)}), f32[16,48,128]{2,1,0:T(8,128)S(1)}, u32[]{:S(2)}, u32[]{:S(2)}) %all-to-all-start) | async-done | bytes 393248 | tf_op jit(solution)/shard_map/all_to_all | solution.py:304
  28.0 0.8 pad_maximum_fusion
  28.8 9.0 %all-to-all-start.1 = ((f32[16,48,128]{2,1,0:T(8,128)}), f32[16,48,128]{2,1,0:T(8,128)S(1)}, u32[]{:S(2)}, u32[]{:S(2)}) async-start(f32[16,48,128]{2,1,0:T(8,128)} %pad_maximum_fusion), calls=%async_computation.1 | async-start | bytes 786432 | tf_op jit(solution)/shard_map/all_to_all | solution.py:304
  37.8 12.3 %all-to-all-done.1 = f32[16,48,128]{2,1,0:T(8,128)S(1)} async-done(((f32[16,48,128]{2,1,0:T(8,128)}), f32[16,48,128]{2,1,0:T(8,128)S(1)}, u32[]{:S(2)}, u32[]{:S(2)}) %all-to-all-start.1) | async-done | bytes 393248 | tf_op jit(solution)/shard_map/all_to_all | solution.py:304
  50.2 16.4 %all_to_all.35.own_ref = f32[16,48,128]{2,1,0:T(8,128)S(1)} all-to-all(f32[16,48,128]{2,1,0:T(8,128)S(1)} %broadcast_in_dim.16), channel_id=1, replica_groups=mesh['row'=16,'pair'=16,'core'=2] {'pair'}, dimensions={0} | all-to-all | bytes 786432 | tf_op jit(solution)/shard_map/all_to_all | solution.py:304
  66.6 6.8 %collective-permute-start.1 = (f32[16,48,128]{2,1,0:T(8,128)S(1)}, f32[16,48,128]{2,1,0:T(8,128)S(1)}, u32[]{:S(2)}, u32[]{:S(2)}) collective-permute-start(f32[16,48,128]{2,1,0:T(8,128)S(1)} %all_to_all.35.own_ref), channel_id=1, source_target_pairs={{0,1},{1,0},{2,3},{3,2},{4,5},{5,4},{6,7},{7,6},{8,9},{9,8},{10,11... | collective-permute-start | bytes 1179656 | tf_op jit(solution)/shard_map/ppermute | solution.py:308
  73.4 1.3 collective-permute-done.1.other_ref
  74.7 2.2 %shard_map.32 = (f32[16,64,128]{2,1,0:T(8,128)}, f32[1024,128]{1,0:T(8,128)S(1)}, f32[256,128]{1,0:T(8,128)S(1)}) custom-call(s32[4]{0:T(128)S(1)} %pad_add_fusion.place, f32[16,48,128]{2,1,0:T(8,128)S(1)} %all_to_all.35.own_ref, f32[16,48,128]{2,1,0:T(8,128)S(1)} %collective-permute-done.1.other_ref, f32[1024,512]{1,0:T(8,128)S(1)} %get-tuple-element.15.matrix_ref, ...), custom_call_target="tpu_custom_call" | custom-call | flops 134217728 | bytes 3670016 | tf_op jit(solution)/shard_map/pallas_call | solution.py:380
  76.9 0.0 copy-done
  76.9 3.9 %all-to-all-start.3 = ((f32[16,64,128]{2,1,0:T(8,128)}), f32[16,64,128]{2,1,0:T(8,128)S(1)}, u32[]{:S(2)}, u32[]{:S(2)}) async-start(f32[16,64,128]{2,1,0:T(8,128)} %get-tuple-element.17), calls=%async_computation.3 | async-start | bytes 1048576 | tf_op jit(solution)/shard_map/all_to_all | solution.py:304
  80.9 13.5 %shard_map.33.factors_ref.band_ref = f32[768,128]{1,0:T(8,128)S(1)} custom-call(f32[256,128]{1,0:T(8,128)S(1)} %get-tuple-element.18.base_ref), custom_call_target="tpu_custom_call" | custom-call | flops 268435456 | bytes 33554432 | tf_op jit(solution)/shard_map/pallas_call | solution.py:295
  94.3 4.0 %all-to-all-done.3.found_ref.chunks_ref = f32[16,64,128]{2,1,0:T(8,128)S(1)} async-done(((f32[16,64,128]{2,1,0:T(8,128)}), f32[16,64,128]{2,1,0:T(8,128)S(1)}, u32[]{:S(2)}, u32[]{:S(2)}) %all-to-all-start.3) | async-done | bytes 524320 | tf_op jit(solution)/shard_map/all_to_all | solution.py:304
  98.4 1.9 %shard_map.34 = (f32[16,40,128]{2,1,0:T(8,128)}, f32[32,128]{1,0:T(8,128)S(1)}) custom-call(s32[4]{0:T(128)S(1)} %pad_add_fusion.place, f32[16,64,128]{2,1,0:T(8,128)S(1)} %all-to-all-done.3.found_ref.chunks_ref, f32[32,128]{1,0:T(8,128)S(1)} %get-tuple-element.33.chunk_ref.panel_ref, f32[32,128]{1,0:T(8,128)S(1)} %get-tuple-element.32.second_ref, ...), custom_call_target="tpu_custom_call" | custom-call | flops 5242880 | bytes 1048576 | tf_op jit(solution)/shard_map/pallas_call | solution.py:390
  100.2 5.0 %all-to-all-start.4 = ((f32[16,40,128]{2,1,0:T(8,128)}), f32[16,40,128]{2,1,0:T(8,128)S(1)}, u32[]{:S(2)}, u32[]{:S(2)}) async-start(f32[16,40,128]{2,1,0:T(8,128)} %get-tuple-element.19), calls=%async_computation.4 | async-start | bytes 655360 | tf_op jit(solution)/shard_map/all_to_all | solution.py:304
  105.3 8.1 %collective-permute-start.2 = (f32[32,128]{1,0:T(8,128)S(1)}, f32[32,128]{1,0:T(8,128)S(1)}, u32[]{:S(2)}, u32[]{:S(2)}) collective-permute-start(f32[32,128]{1,0:T(8,128)S(1)} %get-tuple-element.21), channel_id=1, source_target_pairs={{256,0},{288,1},{320,2},{352,3},{384,4},{416,5},{448,6},{480,7},{0... | collective-permute-start | bytes 49160 | tf_op jit(solution)/shard_map/ppermute | solution.py:324
  113.4 8.1 %collective-permute-done.2.scaled_ref = f32[32,128]{1,0:T(8,128)S(1)} collective-permute-done((f32[32,128]{1,0:T(8,128)S(1)}, f32[32,128]{1,0:T(8,128)S(1)}, u32[]{:S(2)}, u32[]{:S(2)}) %collective-permute-start.2) | collective-permute-done | bytes 16416 | tf_op jit(solution)/shard_map/ppermute | solution.py:324
  121.5 0.0 all-to-all-done.4.found_ref.cols_ref
  121.5 10.8 %all_to_all.36.part_ref = f32[16,40,128]{2,1,0:T(8,128)S(1)} all-to-all(f32[16,40,128]{2,1,0:T(8,128)S(1)} %shard_map.35), channel_id=1, replica_groups=mesh['row'=16,'pair'=16,'core'=2] {'pair'}, dimensions={0} | all-to-all | bytes 655360 | tf_op jit(solution)/shard_map/all_to_all | solution.py:304
  132.3 0.7 shard_map.36
  133.0 5.9 %collective-permute-start.3 = (f32[16,32,128]{2,1,0:T(8,128)S(1)}, f32[16,32,128]{2,1,0:T(8,128)S(1)}, u32[]{:S(2)}, u32[]{:S(2)}) collective-permute-start(f32[16,32,128]{2,1,0:T(8,128)S(1)} %get-tuple-element.24.own_ref), channel_id=1, source_target_pairs={{0,1},{1,0},{2,3},{3,2},{4,5},{5,4},{6,7},{7,6},{8,9},{9,8},{10,11... | collective-permute-start | bytes 786440 | tf_op jit(solution)/shard_map/ppermute | solution.py:308
  138.9 5.9 %all-to-all-start.6 = ((f32[32,8,128]{2,1,0:T(8,128)}), f32[32,8,128]{2,1,0:T(8,128)S(1)}, u32[]{:S(2)}, u32[]{:S(2)}) async-start(f32[32,8,128]{2,1,0:T(8,128)} %get-tuple-element.22.ready_ref), calls=%async_computation.6 | async-start | bytes 262144 | tf_op jit(solution)/shard_map/all_to_all | solution.py:304
  144.9 2.3 %shard_map.37 = (f32[1024,128]{1,0:T(8,128)}, f32[512,128]{1,0:T(8,128)S(1)}, bf16[512,128]{1,0:T(8,128)(2,1)S(1)}, bf16[512,128]{1,0:T(8,128)(2,1)S(1)}) custom-call(s32[4]{0:T(128)S(1)} %pad_add_fusion.place, f32[1024,128]{1,0:T(8,128)S(1)} %get-tuple-element.20.panel_ref, f32[16,64,128]{2,1,0:T(8,128)S(1)} %all-to-all-done.3.found_ref.chunks_ref, ...), custom_call_target="tpu_custom_call" | custom-call | flops 67108864 | bytes 1048576 | tf_op jit(solution)/shard_map/pallas_call | solution.py:415
  147.2 8.5 %all-to-all-done.6.coupling_ref = f32[32,8,128]{2,1,0:T(8,128)S(1)} async-done(((f32[32,8,128]{2,1,0:T(8,128)}), f32[32,8,128]{2,1,0:T(8,128)S(1)}, u32[]{:S(2)}, u32[]{:S(2)}) %all-to-all-start.6) | async-done | bytes 131104 | tf_op jit(solution)/shard_map/all_to_all | solution.py:304
  155.6 0.0 collective-permute-done.3.other_ref
  155.6 0.0 copy-start.1
  155.6 1.0 copy-done.1
  156.7 4.7 %shard_map.38 = f32[1024,4,128]{2,1,0:T(4,128)} custom-call(s32[4]{0:T(128)S(1)} %pad_add_fusion.place, f32[1024,512]{1,0:T(8,128)} %copy-done, f32[16,40,128]{2,1,0:T(8,128)S(1)} %all-to-all-done.4.found_ref.cols_ref, f32[512,128]{1,0:T(8,128)S(1)} %get-tuple-element.23.reflect_cols_ref, f32[16,32,128]{2,1,0:T(8,128)S(1)} %get-tuple-element.24.own_ref, ...), custom_call_target="tpu_custom_call" | custom-call | flops 268435456 | bytes 4194304 | tf_op jit(solution)/shard_map/pallas_call | solution.py:424
  (9 shorter events, 0.1 us)
Async XLA Ops:
  2.5 9.2 %collective-permute-start = (f32[512,128]{1,0:T(8,128)S(1)}, f32[512,128]{1,0:T(8,128)S(1)}, u32[]{:S(2)}, u32[]{:S(2)}) collective-permute-start(f32[512,128]{1,0:T(8,128)S(1)} %get-tuple-element.30), channel_id=1, source_target_pairs={{0,1},{32,33},{64,65},{96,97},{128,129},{160,161},{192,193},{224,2... | collective-permute-start | bytes 786440 | tf_op jit(solution)/shard_map/ppermute | solution.py:354
  13.4 14.6 %all-to-all-start = ((f32[16,48,128]{2,1,0:T(8,128)}), f32[16,48,128]{2,1,0:T(8,128)S(1)}, u32[]{:S(2)}, u32[]{:S(2)}) async-start(f32[16,48,128]{2,1,0:T(8,128)} %shard_map.31), calls=%async_computation | async-start | bytes 786432 | tf_op jit(solution)/shard_map/all_to_all | solution.py:304
  20.3 56.6 %copy-start = (f32[1024,512]{1,0:T(8,128)}, f32[1024,512]{1,0:T(8,128)S(1)}, u32[]{:S(2)}) copy-start(f32[1024,512]{1,0:T(8,128)S(1)} %get-tuple-element.15.matrix_ref) | copy-start | bytes 6291460
  28.8 21.4 %all-to-all-start.1 = ((f32[16,48,128]{2,1,0:T(8,128)}), f32[16,48,128]{2,1,0:T(8,128)S(1)}, u32[]{:S(2)}, u32[]{:S(2)}) async-start(f32[16,48,128]{2,1,0:T(8,128)} %pad_maximum_fusion), calls=%async_computation.1 | async-start | bytes 786432 | tf_op jit(solution)/shard_map/all_to_all | solution.py:304
  66.6 8.1 %collective-permute-start.1 = (f32[16,48,128]{2,1,0:T(8,128)S(1)}, f32[16,48,128]{2,1,0:T(8,128)S(1)}, u32[]{:S(2)}, u32[]{:S(2)}) collective-permute-start(f32[16,48,128]{2,1,0:T(8,128)S(1)} %all_to_all.35.own_ref), channel_id=1, source_target_pairs={{0,1},{1,0},{2,3},{3,2},{4,5},{5,4},{6,7},{7,6},{8,9},{9,8},{10,11... | collective-permute-start | bytes 1179656 | tf_op jit(solution)/shard_map/ppermute | solution.py:308
  76.9 21.5 %all-to-all-start.3 = ((f32[16,64,128]{2,1,0:T(8,128)}), f32[16,64,128]{2,1,0:T(8,128)S(1)}, u32[]{:S(2)}, u32[]{:S(2)}) async-start(f32[16,64,128]{2,1,0:T(8,128)} %get-tuple-element.17), calls=%async_computation.3 | async-start | bytes 1048576 | tf_op jit(solution)/shard_map/all_to_all | solution.py:304
  100.2 21.2 %all-to-all-start.4 = ((f32[16,40,128]{2,1,0:T(8,128)}), f32[16,40,128]{2,1,0:T(8,128)S(1)}, u32[]{:S(2)}, u32[]{:S(2)}) async-start(f32[16,40,128]{2,1,0:T(8,128)} %get-tuple-element.19), calls=%async_computation.4 | async-start | bytes 655360 | tf_op jit(solution)/shard_map/all_to_all | solution.py:304
  105.3 16.2 %collective-permute-start.2 = (f32[32,128]{1,0:T(8,128)S(1)}, f32[32,128]{1,0:T(8,128)S(1)}, u32[]{:S(2)}, u32[]{:S(2)}) collective-permute-start(f32[32,128]{1,0:T(8,128)S(1)} %get-tuple-element.21), channel_id=1, source_target_pairs={{256,0},{288,1},{320,2},{352,3},{384,4},{416,5},{448,6},{480,7},{0... | collective-permute-start | bytes 49160 | tf_op jit(solution)/shard_map/ppermute | solution.py:324
  133.0 22.7 %collective-permute-start.3 = (f32[16,32,128]{2,1,0:T(8,128)S(1)}, f32[16,32,128]{2,1,0:T(8,128)S(1)}, u32[]{:S(2)}, u32[]{:S(2)}) collective-permute-start(f32[16,32,128]{2,1,0:T(8,128)S(1)} %get-tuple-element.24.own_ref), channel_id=1, source_target_pairs={{0,1},{1,0},{2,3},{3,2},{4,5},{5,4},{6,7},{7,6},{8,9},{9,8},{10,11... | collective-permute-start | bytes 786440 | tf_op jit(solution)/shard_map/ppermute | solution.py:308
  138.9 16.7 %all-to-all-start.6 = ((f32[32,8,128]{2,1,0:T(8,128)}), f32[32,8,128]{2,1,0:T(8,128)S(1)}, u32[]{:S(2)}, u32[]{:S(2)}) async-start(f32[32,8,128]{2,1,0:T(8,128)} %get-tuple-element.22.ready_ref), calls=%async_computation.6 | async-start | bytes 262144 | tf_op jit(solution)/shard_map/all_to_all | solution.py:304
  155.6 1.0 copy-start.1
